TPU v7x, 128 devices: a whole 4x4x4 slice. The times are simulated.
128 devices in a mesh: parts: 1, seq: 16 (over y, x), head: 8 (over z, core).
Axes of the slice: x: 4, y: 4, z: 4, core: 2. Of those that a mesh axis runs over, the one named last changes fastest.
Arguments:
- prompt_x: bfloat16 [2048, 8192], P(('parts', 'seq'), 'head'), may hold values from -6 to 6
- prompt_b: bfloat16 [2048, 1024], P(('parts', 'seq'), 'head'), may hold values from -0.5 to 0.5
- prompt_dt: float32 [128, 2048], P('head', ('parts', 'seq')), may hold values from 0.5 to 2
- branch_x: bfloat16 [2048, 8192], P(('parts', 'seq'), 'head'), may hold values from -6 to 6
- branch_b: bfloat16 [2048, 1024], P(('parts', 'seq'), 'head'), may hold values from -0.5 to 0.5
- branch_c: bfloat16 [2048, 1024], P(('parts', 'seq'), 'head'), may hold values from -0.5 to 0.5
- branch_z: bfloat16 [2048, 8192], P(('parts', 'seq'), 'head'), may hold values from -6 to 6
- branch_dt: float32 [128, 2048], P('head', ('parts', 'seq')), may hold values from 0.5 to 2
- a_rate: float32 [128], P('head'), may hold values from 0.00024414062 to 0.05
- d_skip: float32 [128], P('head'), may hold values from 0.5 to 1.5
- norm_gain: float32 [8192], P('head'), may hold values from 0.5 to 1.5
- branch_parent: int32 [64], P(('parts', 'seq')), may hold values from 0 to 15
- group_ids: int32 [2048], P(('parts', 'seq')), may hold values from 0 to 7, as said below
- returns: float32 [2048], P(('parts', 'seq')), may hold values from -6 to 6
- out_grad: bfloat16 [2048, 8192], P(('parts', 'seq'), 'head'), may hold values from -6 to 6
Outputs:
- branch_out: bfloat16 [2048, 8192], P(('parts', 'seq'), 'head')
- branch_grad: bfloat16 [2048, 8192], P(('parts', 'seq'), 'head')
- prompt_grad: float32 [2048, 8192], P(('parts', 'seq'), 'head')
Inputs may be any that keep to these rules, and one draw needn't show every extreme that they name: `group_ids`: exactly one advantage group other than 0 and 7 holds no token; which one varies.
All inputs are finite; a program needn't handle non-finite values.
Results may differ from a plain program's by a relative error of at most 0.0095.
Values may be sent and summed in bfloat16 or wider, within the bound.
A program may use at most 128 MiB of HBM per device.

v0:
```python
import jax
import jax.numpy as jnp
from jax import lax
from jax.sharding import PartitionSpec as P

HEADS = 128
HEAD_DIM = 64
STATE = 128
GROUPS = 8
BLOCK = 128
SEG = 32
ADV_GROUPS = 8


EPSILON = 1e-05
PRECISE = lax.Precision.HIGHEST


def prefix(value, axis, join, neutral, backward):
    count, mine = (lax.axis_size(axis), lax.axis_index(axis))
    pieces = jax.tree.map(lambda part: lax.all_gather(part, axis), value)
    if backward:
        pieces = jax.tree.map(lambda part: part[::-1], pieces)
        mine = count - 1 - mine
    so_far = jax.tree.map(
        lambda part, zero: jnp.full_like(part, 0) + jnp.asarray(zero, part.dtype), value, neutral
    )

    def turn(position, so_far):
        longer = join(so_far, jax.tree.map(lambda part: part[position], pieces))
        return jax.tree.map(lambda new, old: jnp.where(position < mine, new, old), longer, so_far)

    return lax.fori_loop(0, count - 1, turn, so_far)


def expand_groups(values, repeat_count):
    rows = values.shape[0]
    grouped = values.astype(jnp.float32).reshape(rows, -1, STATE)
    return jnp.repeat(grouped, repeat_count, axis=1)


def block_weights(step_sizes, rates, block):
    heads, length = step_sizes.shape
    logs = (step_sizes * (-rates)[:, None]).reshape(heads, length // block, block)
    running = jnp.cumsum(logs, axis=2)
    totals = running[:, :, -1]
    tails = jnp.exp(totals[:, :, None] - running) * step_sizes.reshape(
        heads, length // block, block
    )
    return (tails, totals)


def block_updates(inputs, projections, step_sizes, rates):
    tails, totals = block_weights(step_sizes, rates, BLOCK)
    heads = step_sizes.shape[0]
    count = totals.shape[1]
    values = inputs.astype(jnp.float32).reshape(count, BLOCK, heads, HEAD_DIM)
    loads = expand_groups(projections, HEADS // GROUPS).reshape(count, BLOCK, heads, STATE)
    weighted = values * jnp.transpose(tails, (1, 2, 0))[..., None]
    updates = jnp.einsum("kqhp,kqhn->khpn", weighted, loads, precision=PRECISE)
    return (updates, tails, totals, loads)


def chain_blocks(updates, totals):

    def advance(carry, item):
        update, total = item
        carry = jnp.exp(total)[:, None, None] * carry + update
        return (carry, carry)

    _, ends = lax.scan(advance, jnp.zeros_like(updates[0]), (updates, totals.T))
    return ends


def back_chain(arriving, totals):

    def retreat(carry, item):
        gradient, decay = carry
        incoming, total = item
        gradient = incoming + decay[:, None, None] * gradient
        return ((gradient, jnp.exp(total)), gradient)

    start = (jnp.zeros_like(arriving[0]), jnp.ones_like(totals[:, 0]))
    _, gradients = lax.scan(retreat, start, (arriving, totals.T), reverse=True)
    return gradients


def prompt_gradient(gradients, tails, loads):
    count = gradients.shape[0]
    heads = gradients.shape[1]
    applied = jnp.einsum("khpn,kqhn->kqhp", gradients, loads, precision=PRECISE)
    applied = applied * jnp.transpose(tails, (1, 2, 0))[..., None]
    return applied.reshape(count * BLOCK, heads * HEAD_DIM)


def branch_forward(inputs, in_proj, out_proj, step_sizes, rates, skips, forks):
    rows = inputs.shape[0]
    heads = step_sizes.shape[0]
    branches = rows // SEG
    logs = (step_sizes * (-rates)[:, None]).reshape(heads, branches, SEG)
    running = jnp.cumsum(logs, axis=2)
    values = inputs.astype(jnp.float32).reshape(branches, SEG, heads, HEAD_DIM)
    loads = expand_groups(in_proj, HEADS // GROUPS).reshape(branches, SEG, heads, STATE)
    reads = expand_groups(out_proj, HEADS // GROUPS).reshape(branches, SEG, heads, STATE)
    differ = running[:, :, :, None] - running[:, :, None, :]
    lower = jnp.arange(SEG, dtype=jnp.int32)[:, None] >= jnp.arange(SEG, dtype=jnp.int32)[None, :]
    decays = jnp.where(lower[None, None], jnp.exp(jnp.minimum(differ, 0.0)), 0.0)
    steps_bt = step_sizes.reshape(heads, branches, SEG)
    scores = jnp.einsum("bthn,bshn->bhts", reads, loads, precision=PRECISE)
    mixing = (
        scores
        * jnp.transpose(decays, (1, 0, 2, 3))
        * jnp.transpose(steps_bt, (1, 0, 2))[:, :, None, :]
    )
    inner = jnp.einsum("bhts,bshp->bthp", mixing, values, precision=PRECISE)
    lift = jnp.transpose(jnp.exp(running), (1, 2, 0))
    carried = jnp.einsum("bthn,bhpn->bthp", reads, forks, precision=PRECISE) * lift[..., None]
    output = inner + carried + skips[None, None, :, None] * values
    return (output.reshape(rows, heads * HEAD_DIM), mixing, lift, reads)


def branch_backward(cotangent, mixing, lift, reads, skips):
    branches, heads = (mixing.shape[0], mixing.shape[1])
    upstream = cotangent.reshape(branches, SEG, heads, HEAD_DIM)
    inputs_grad = jnp.einsum("bhts,bthp->bshp", mixing, upstream, precision=PRECISE)
    inputs_grad = inputs_grad + skips[None, None, :, None] * upstream
    state_grads = jnp.einsum(
        "bthn,bthp->bhpn", reads * lift[..., None], upstream, precision=PRECISE
    )
    return (inputs_grad.reshape(branches * SEG, heads * HEAD_DIM).astype(jnp.bfloat16), state_grads)


def group_table(group_ids):
    return (group_ids[:, None] == jnp.arange(ADV_GROUPS, dtype=jnp.int32)[None, :]).astype(
        jnp.float32
    )


def group_terms(group_ids, returns):
    table = group_table(group_ids)
    counts = jnp.sum(table, axis=0)
    sums = jnp.dot(returns, table, precision=PRECISE)
    squares = jnp.dot(returns * returns, table, precision=PRECISE)
    return (counts, sums, squares)


def advantages(stats, group_ids, returns):
    counts, sums, squares = stats
    table = group_table(group_ids)
    floor_count = jnp.maximum(counts, 1.0)
    means = sums / floor_count
    spread = jnp.sqrt(squares / floor_count - means * means + 1.0)
    token_mean = jnp.dot(table, means, precision=PRECISE)
    token_spread = jnp.dot(table, spread, precision=PRECISE)
    return (returns - token_mean) / token_spread


def joined(earlier, later):
    return (earlier[0] * later[0], later[0][:, None, None] * earlier[1] + later[1])


def local(
    prompt_x,
    prompt_b,
    prompt_dt,
    branch_x,
    branch_b,
    branch_c,
    branch_z,
    branch_dt,
    a_rate,
    d_skip,
    norm_gain,
    branch_parent,
    group_ids,
    returns,
    out_grad,
):
    branches = branch_parent.shape[0]
    updates, tails, totals, loads = block_updates(prompt_x, prompt_b, prompt_dt, a_rate)
    blocks = totals.shape[1]
    local_ends = chain_blocks(updates, totals)
    span = jnp.exp(jnp.sum(totals, axis=1))
    identity = (jnp.ones_like(span), jnp.zeros_like(local_ends[0]))
    _, entering = prefix((span, local_ends[-1]), "seq", joined, identity, False)
    rising = jnp.exp(jnp.cumsum(totals, axis=1))
    ends = local_ends + rising.T[:, :, None, None] * entering[None]
    empty = jnp.zeros((branches,) + ends.shape[1:], jnp.float32)
    piece = lax.all_gather(ends, "seq", axis=0, tiled=True)
    positions = jnp.arange(piece.shape[0], dtype=jnp.int32)
    chosen = (branch_parent[:, None] == positions[None, :]).astype(jnp.float32)
    forks = empty + jnp.einsum("bm,mhpn->bhpn", chosen, piece, precision=PRECISE)
    output, mixing, lift, reads = branch_forward(
        branch_x, branch_b, branch_c, branch_dt, a_rate, d_skip, forks
    )
    opened = jax.nn.silu(branch_z.astype(jnp.float32))
    gated = output * opened
    total_sq = lax.psum(jnp.sum(gated * gated, axis=1), "head")
    scale = lax.rsqrt(total_sq / (HEADS * HEAD_DIM) + EPSILON)
    branch_out = (gated * scale[:, None] * norm_gain[None, :]).astype(jnp.bfloat16)
    stats = lax.psum(group_terms(group_ids, returns), "seq")
    weights = advantages(stats, group_ids, returns)
    pushed = out_grad.astype(jnp.float32) * weights[:, None] * norm_gain[None, :]
    along = lax.psum(jnp.sum(pushed * gated, axis=1), "head")
    cotangent = (
        scale[:, None] * pushed
        - gated * (scale * scale * scale * along / (HEADS * HEAD_DIM))[:, None]
    ) * opened
    branch_grad, state_grads = branch_backward(cotangent, mixing, lift, reads, d_skip)
    positions = jnp.arange(blocks * lax.axis_size("seq"), dtype=jnp.int32)
    chosen = (branch_parent[None, :] == positions[:, None]).astype(jnp.float32)
    arriving = lax.psum_scatter(
        jnp.einsum("mb,bhpn->mhpn", chosen, state_grads, precision=PRECISE),
        "seq",
        scatter_dimension=0,
        tiled=True,
    )
    local_grads = back_chain(arriving, totals)
    span = jnp.exp(jnp.sum(totals, axis=1))
    start_grad = jnp.exp(totals[:, 0])[:, None, None] * local_grads[0]
    identity = (jnp.ones_like(span), jnp.zeros_like(start_grad))
    _, leaving = prefix((span, start_grad), "seq", joined, identity, True)
    after = jnp.exp(jnp.sum(totals, axis=1)[:, None] - jnp.cumsum(totals, axis=1))
    gradients = local_grads + after.T[:, :, None, None] * leaving[None]
    prompt_grad = prompt_gradient(gradients, tails, loads)
    return (branch_out, branch_grad, prompt_grad)


def solution(mesh):
    placed = (
        P(("parts", "seq"), "head"),
        P(("parts", "seq"), "head"),
        P("head", ("parts", "seq")),
        P(("parts", "seq"), "head"),
        P(("parts", "seq"), "head"),
        P(("parts", "seq"), "head"),
        P(("parts", "seq"), "head"),
        P("head", ("parts", "seq")),
        P("head"),
        P("head"),
        P("head"),
        P(("parts", "seq")),
        P(("parts", "seq")),
        P(("parts", "seq")),
        P(("parts", "seq"), "head"),
    )
    return jax.shard_map(
        local,
        mesh=mesh,
        in_specs=placed,
        out_specs=(
            P(("parts", "seq"), "head"),
            P(("parts", "seq"), "head"),
            P(("parts", "seq"), "head"),
        ),
        check_vma=False,
    )
```

profile of v0, /device:TPU:0, one launch (start us, length us, event | category | flops | bytes accessed | tf_op | source)
XLA Modules:
  0.0 417.1 jit_solution(16760622434486891717)
XLA Ops:
  7.3 0.7 neg.8
  8.0 0.8 broadcast_multiply_fusion.1
  9.3 0.8 fusion.47
  10.0 0.8 convert_element_type.28
  10.8 1.1 copy.70
  11.9 1.7 convolution_add_fusion
  13.8 1.3 dynamic-slice.1
  16.0 0.8 convert_reduce_fusion
  16.7 0.8 convolution_bitcast_fusion.6
  17.5 0.8 convolution_bitcast_fusion.4
  18.3 41.0 %all-reduce.2 = (f32[256]{0:T(256)S(1)}, f32[8]{0:T(128)S(1)}, f32[8]{0:T(128)S(1)}, f32[8]{0:T(128)S(1)}) all-reduce(f32[256]{0:T(256)S(1)} %dynamic-update-slice, f32[8]{0:T(128)S(1)} %convolution_bitcast_fusion.6, f32[8]{0:T(128)S(1)} %convert_reduce_fusion, ...), channel_id=2, replica_groups=mesh['parts'=1,'seq'=16,'head'=8] {'seq'}, use_global_device_ids=true, to_apply=%add | all-reduce | flops 280 | bytes 2240
  60.0 27.1 %all-gather.9.cloned.1.call-done = f32[256,64,128]{2,1,0:T(8,128)} async-done(((f32[16,64,128]{2,1,0:T(8,128)}), f32[256,64,128]{2,1,0:T(8,128)}) %all-gather.9.cloned.1.call-update) | async-done | bytes 8388624 | tf_op jit(solution)/shard_map/all_gather | solution.py:21
  87.1 18.2 %while.18 = (s32[]{:T(128)}, f32[16,64,128]{2,1,0:T(8,128)S(1)}, s32[]{:T(128)}, f32[16,16]{1,0:T(8,128)S(1)}, f32[16,16,64,128]{3,2,1,0:T(8,128)}, /*index=5*/s32[]{:T(128)}, s32[]{:T(128)}) while((s32[]{:T(128)}, f32[16,64,128]{2,1,0:T(8,128)S(1)}, s32[]{:T(128)}, f32[16,16]{1,0:T(8,128)S(1)}, f32[16,16,64,128]{3,2,1,0:T(8,128)}, ...), condition=%wide.region_3.4_spmd.clone, body=%wide.region_2.3_spmd.clone.sunk | while | flops 524292 | bytes 1573169 | solution.py:33
  87.1 1.2 fusion.74
  88.3 1.2 fusion.74
  89.5 1.2 fusion.74
  90.8 1.2 fusion.74
  92.0 1.2 fusion.74
  93.2 1.2 fusion.74
  94.4 1.2 fusion.74
  95.6 1.2 fusion.74
  96.8 1.2 fusion.74
  98.1 1.2 fusion.74
  99.3 1.2 fusion.74
  100.5 1.2 fusion.74
  101.7 1.2 fusion.74
  102.9 1.2 fusion.74
  104.2 1.2 fusion.74
  105.4 0.9 multiply_add_fusion
  106.5 0.9 reduce_window_sum.31
  108.2 1.8 fusion.15
  110.0 0.7 convolution_bitcast_fusion.1
  110.7 66.0 %all-gather.11.cloned.1.call-done = f32[256,64,128]{2,1,0:T(8,128)} async-done(((f32[16,64,128]{2,1,0:T(8,128)}), f32[256,64,128]{2,1,0:T(8,128)}) %all-gather.11.cloned.1.call-update) | async-done | bytes 8388624 | tf_op jit(solution)/shard_map/all_gather | solution.py:189
  176.7 11.0 %fusion.2 = f32[4,16,64,128]{3,0,2,1:T(4,128)S(1)} fusion(f32[16,16,64,128]{3,2,1,0:T(8,128)} %bitcast.120, s32[4]{0:T(128)S(1)} %copy-done.15), kind=kOutput, calls=%fused_computation.6 | convolution fusion | flops 100663360 | bytes 10485776 | tf_op jit(solution)/shard_map/bm,mhpn->bhpn/dot_general | solution.py:192
  187.7 3.6 fusion.19
  192.7 14.8 %all-reduce.3 = (f32[128]{0:T(128)S(1)}, f32[128]{0:T(128)S(1)}) all-reduce(f32[128]{0:T(128)S(1)} %get-tuple-element.288, f32[128]{0:T(128)S(1)} %get-tuple-element.287), channel_id=1, replica_groups=mesh['parts'=1,'seq'=16,'head'=8] {'head'}, use_global_device_ids=true, to_apply=%region_5.6 | all-reduce | flops 256 | bytes 2048 | tf_op jit(solution)/shard_map/psum | solution.py:198
  207.5 2.0 subtract_multiply_fusion
  209.8 4.5 %fusion.26 = f32[4,16,64,128]{3,2,1,0:T(8,128)S(1)} fusion(f32[4,32,16,64]{3,2,1,0:T(8,128)S(1)} %reshape.151, f32[4,32,16]{1,2,0:T(8,128)} %copy-done.4, f32[4,32,128]{2,1,0:T(8,128)S(1)} %convert.4), kind=kOutput, calls=%fused_computation.31 | convolution fusion | flops 201588736 | bytes 2695168 | tf_op jit(solution)/shard_map/bthn,bthp->bhpn/dot_general | solution.py:127
  214.3 5.7 %fusion.4 = f32[16,16,64,128]{3,0,2,1:T(8,128)S(1)} fusion(f32[4,16,64,128]{3,2,1,0:T(8,128)S(1)} %fusion.26, s32[4]{0:T(128)} %param.30), kind=kOutput, calls=%fused_computation.8 | convolution fusion | flops 100663360 | bytes 10485776 | tf_op jit(solution)/shard_map/mb,bhpn->mhpn/dot_general | solution.py:213
  220.0 6.0 %copy.81 = f32[16,16,64,128]{3,2,1,0:T(8,128)} copy(f32[16,16,64,128]{3,0,2,1:T(8,128)S(1)} %fusion.4) | data formatting | bytes 16777216 | tf_op jit(solution)/shard_map/mb,bhpn->mhpn/dot_general | solution.py:213
  226.1 82.2 %reduce-scatter.4.cloned.1.call-done = f32[1,16,64,128]{3,2,1,0:T(8,128)} async-done(((f32[16,16,64,128]{3,2,1,0:T(8,128)}), f32[1,16,64,128]{3,2,1,0:T(8,128)}) %reduce-scatter.4.cloned.1.call-update) | async-done | bytes 524304
  308.3 1.9 broadcast_multiply_fusion
  310.3 2.3 fusion.22
  312.8 1.1 convert_element_type.34
  313.9 67.0 %all-gather.7.cloned.1.call-done = f32[16,16,64,128]{3,2,1,0:T(8,128)} async-done(((f32[1,16,64,128]{3,2,1,0:T(8,128)}), f32[16,16,64,128]{3,2,1,0:T(8,128)}) %all-gather.7.cloned.1.call-update) | async-done | bytes 8388624 | tf_op jit(solution)/shard_map/all_gather | solution.py:21
  380.9 8.3 %rev.7 = f32[16,16,64,128]{3,2,1,0:T(8,128)} reverse(f32[16,16,64,128]{3,2,1,0:T(8,128)} %all-gather.7.cloned.1.call-done), dimensions={0} | reverse | bytes 16777216 | tf_op jit(solution)/shard_map/rev | solution.py:23
  389.2 18.3 %while.19 = (s32[]{:T(128)}, f32[16,64,128]{2,1,0:T(8,128)S(1)}, s32[]{:T(128)}, f32[16,16]{1,0:T(8,128)S(1)}, f32[16,16,64,128]{3,2,1,0:T(8,128)}, /*index=5*/s32[]{:T(128)}, s32[]{:T(128)}) while((s32[]{:T(128)}, f32[16,64,128]{2,1,0:T(8,128)S(1)}, s32[]{:T(128)}, f32[16,16]{1,0:T(8,128)S(1)}, f32[16,16,64,128]{3,2,1,0:T(8,128)}, ...), condition=%wide.region_14.15_spmd.clone, body=%wide.region_13.14_spmd.clone.sunk | while | flops 524292 | bytes 1573169 | solution.py:33
  389.2 1.2 fusion.75
  390.4 1.2 fusion.75
  391.6 1.2 fusion.75
  392.9 1.2 fusion.75
  394.1 1.2 fusion.75
  395.3 1.2 fusion.75
  396.5 1.2 fusion.75
  397.7 1.2 fusion.75
  399.0 1.2 fusion.75
  400.2 1.2 fusion.75
  401.4 1.2 fusion.75
  402.6 1.2 fusion.75
  403.9 1.2 fusion.75
  405.1 1.2 fusion.75
  406.3 1.2 fusion.75
  407.5 2.1 fusion.23
  409.6 1.0 copy.82
  (104 shorter events, 4.6 us)
Async XLA Ops:
  7.2 99.2 %copy-start.8 = (f32[16,128]{1,0:T(8,128)S(1)}, f32[16,128]{1,0:T(8,128)}, u32[]{:S(2)}) copy-start(f32[16,128]{1,0:T(8,128)} %param.26) | copy-start | bytes 24580
  7.2 100.7 %copy-start.17 = (s32[128]{0:T(128)S(1)}, s32[128]{0:T(128)}, u32[]{:S(2)}) copy-start(s32[128]{0:T(128)} %param.31) | copy-start | bytes 1540
  7.2 100.9 %copy-start.18 = (f32[128]{0:T(128)S(1)}, f32[128]{0:T(128)}, u32[]{:S(2)}) copy-start(f32[128]{0:T(128)} %param.32) | copy-start | bytes 1540
  7.2 100.3 %copy-start.6 = (bf16[128,128]{1,0:T(8,128)(2,1)S(1)}, bf16[128,128]{1,0:T(8,128)(2,1)}, u32[]{:S(2)}) copy-start(bf16[128,128]{1,0:T(8,128)(2,1)} %param.24) | copy-start | bytes 98308
  7.2 100.3 %copy-start.7 = (bf16[128,128]{1,0:T(8,128)(2,1)S(1)}, bf16[128,128]{1,0:T(8,128)(2,1)}, u32[]{:S(2)}) copy-start(bf16[128,128]{1,0:T(8,128)(2,1)} %param.23) | copy-start | bytes 98308
  7.2 100.3 %copy-start.5 = (bf16[128,1024]{1,0:T(8,128)(2,1)S(1)}, bf16[128,1024]{1,0:T(8,128)(2,1)}, u32[]{:S(2)}) copy-start(bf16[128,1024]{1,0:T(8,128)(2,1)} %param.22) | copy-start | bytes 786436
  7.2 79.9 %all-gather.9.cloned.1.call-start = ((), (), s32[]{:S(2)}) async-start(), calls=%async_computation.2 | async-start | bytes 8912896 | tf_op jit(solution)/shard_map/all_gather | solution.py:21
  9.2 77.9 %copy-start.10 = (f32[16]{0:T(128)}, f32[16]{0:T(128)S(1)}, u32[]{:S(2)}) copy-start(f32[16]{0:T(128)S(1)} %get-tuple-element.289) | copy-start | bytes 196
  13.7 91.7 %copy-start = (f32[16,64,128]{2,1,0:T(8,128)S(1)}, f32[16,64,128]{2,1,0:T(8,128)}, u32[]{:S(2)}) copy-start(f32[16,64,128]{2,1,0:T(8,128)} %convolution_add_fusion) | copy-start | bytes 1572868
  13.7 163.0 %copy-start.15 = (s32[4]{0:T(128)S(1)}, s32[4]{0:T(128)}, u32[]{:S(2)}) copy-start(s32[4]{0:T(128)} %param.30) | copy-start | bytes 52
  13.7 163.0 %all-gather.11.cloned.1.call-start = ((), (), s32[]{:S(2)}) async-start(), calls=%async_computation.3 | async-start | bytes 8912896 | tf_op jit(solution)/shard_map/all_gather | solution.py:189
  106.3 81.4 %copy-start.13 = (f32[16]{0:T(128)S(1)}, f32[16]{0:T(128)}, u32[]{:S(2)}) copy-start(f32[16]{0:T(128)} %param.28) | copy-start | bytes 196
  106.3 202.0 %reduce-scatter.4.cloned.1.call-start = ((), (), s32[]{:S(2)}) async-start(), calls=%async_computation.4 | async-start | bytes 8912896
  108.2 84.1 %copy-start.12 = (f32[128]{0:T(128)}, f32[128]{0:T(128)S(1)}, u32[]{:S(2)}) copy-start(f32[128]{0:T(128)S(1)} %fusion.25) | copy-start | bytes 1540
  108.2 83.1 %copy-start.4 = (f32[4,32,16]{1,2,0:T(8,128)}, f32[4,32,16]{1,2,0:T(8,128)S(1)}, u32[]{:S(2)}) copy-start(f32[4,32,16]{1,2,0:T(8,128)S(1)} %exponential_bitcast_fusion) | copy-start | bytes 24580
  176.7 15.6 %copy-start.2 = (bf16[128,1024]{1,0:T(8,128)(2,1)S(1)}, bf16[128,1024]{1,0:T(8,128)(2,1)}, u32[]{:S(2)}) copy-start(bf16[128,1024]{1,0:T(8,128)(2,1)} %param.33) | copy-start | bytes 786436
  176.7 15.6 %copy-start.3 = (bf16[128,1024]{1,0:T(8,128)(2,1)S(1)}, bf16[128,1024]{1,0:T(8,128)(2,1)}, u32[]{:S(2)}) copy-start(bf16[128,1024]{1,0:T(8,128)(2,1)} %param.25) | copy-start | bytes 786436
  176.7 15.6 %copy-start.9 = (f32[1024]{0:T(1024)S(1)}, f32[1024]{0:T(1024)}, u32[]{:S(2)}) copy-start(f32[1024]{0:T(1024)} %param.29) | copy-start | bytes 12292
  226.0 82.3 %copy-start.11 = (f32[16]{0:T(128)S(1)}, f32[16]{0:T(128)}, u32[]{:S(2)}) copy-start(f32[16]{0:T(128)} %copy-done.10) | copy-start | bytes 196
  226.0 84.2 %copy-start.14 = (f32[16]{0:T(128)S(1)}, f32[16]{0:T(128)}, u32[]{:S(2)}) copy-start(f32[16]{0:T(128)} %param.28) | copy-start | bytes 196
  226.1 154.9 %all-gather.7.cloned.1.call-start = ((), (), s32[]{:S(2)}) async-start(), calls=%async_computation.1 | async-start | bytes 8912896 | tf_op jit(solution)/shard_map/all_gather | solution.py:21
  313.9 93.6 %copy-start.1 = (f32[1,16,64,128]{3,2,1,0:T(8,128)S(1)}, f32[1,16,64,128]{3,2,1,0:T(8,128)}, u32[]{:S(2)}) copy-start(f32[1,16,64,128]{3,2,1,0:T(8,128)} %reduce-scatter.4.cloned.1.call-done) | copy-start | bytes 1572868
  313.9 93.6 %copy-start.16 = (f32[16]{0:T(128)S(1)}, f32[16]{0:T(128)}, u32[]{:S(2)}) copy-start(f32[16]{0:T(128)} %get-tuple-element.320) | copy-start | bytes 196
Sparse Core Ops, SparseCore 0:
  13.8 73.2 all-gather.8
  106.4 70.2 all-gather.10
  226.2 82.0 reduce-scatter.3
  310.9 70.0 all-gather.6
where the time goes:
time: 420 us; the launch traced here: 417 us
  waiting for transfers between devices  242 us (58%)
  blocking collectives  55.8 us (13%)
  other arithmetic  46 us (11%)
  matrix products  35.3 us (8%)
  local copies, waits for them, and re-layouts  21.6 us (5%)
  between operations  14.8 us (4%)
    all_gather x2, waiting for transfers between devices, prefix(): pieces = jax.tree.map(lambda part: lax.all_gather(part, axis), value)  94.2 us
    unnamed x5, waiting for transfers between devices  82.3 us
    all_gather x1, waiting for transfers between devices, local(): piece = lax.all_gather(ends, 'seq', axis=0, tiled=True)  66 us
    unnamed x1, blocking collectives  41 us
    select_n x30, other arithmetic, turn(): jnp.where(position < mine, new, old)  35.3 us
    psum x1, blocking collectives, local(): total_sq = lax.psum(jnp.sum(gated * gated, axis=1), 'head')  14.8 us
    dot_general x1, matrix products, local(): jnp.einsum('bm,mhpn->bhpn', chosen, piece, precision=PRECISE)  11 us
  transfers between devices with their start and end apart: 4, of which 4 were waited for; matrix products, arithmetic and copies ran while one was open for 3% of the time, Pallas kernels for 0%

commit v1 on v0

v1 whole, which is shorter than its diff:
```python
import functools

import jax
import jax.numpy as jnp
from jax import lax
from jax.experimental import pallas as pl
from jax.experimental.pallas import tpu as pltpu
from jax.sharding import PartitionSpec as P

HEADS = 128
HEAD_DIM = 64
STATE = 128
BLOCK = 128
SEG = 32
NB = 4
EPSILON = 1e-05
SIDE = 4
LOCAL_HEADS = 16
CH = 1024
HALF = 512
NCH = 2
CW = HALF // NCH
MESH_ID = pl.DeviceIdType.MESH
F32 = jnp.float32
BF16 = jnp.bfloat16
HIGH = lax.Precision.HIGHEST


def iota(shape, dim):
    return lax.broadcasted_iota(jnp.int32, shape, dim)


def column(row, n):
    eye = iota((n, n), 0) == iota((n, n), 1)
    return jnp.sum(jnp.where(eye, jnp.broadcast_to(row, (n, n)), 0.0), axis=1, keepdims=True)


def split(v):
    high = v.astype(BF16).astype(F32)
    return high, v - high


def mm(a, b):
    return jnp.dot(a, b, preferred_element_type=F32)


def rows_to_tokens(w, width):
    return jnp.concatenate([jnp.broadcast_to(w[b : b + 1], (SEG, width)) for b in range(NB)], axis=0)


def kernel(
    px, pb, pdt, bx, bb, bc, bz, bdt, rate, skip, gain, par, gid, ret, og,
    out_o, grad_o, prompt_o,
    pk, ar, ug, cg, ct, yp, yr, dg, gp, gr, acc, wt, tail_e, lift_e, einv_e, smat, y_s, gated_s, sz_s, dy_s,
    pk_s, pk_r, ar_s, ar_r, u_s, u_r, c_s, c_r, y_ss, y_rs, d_s, d_r, g_s, g_r,
):
    seq = lax.axis_index("seq")
    head = lax.axis_index("head")
    yi, xi = seq // SIDE, seq % SIDE

    barrier = pltpu.get_barrier_semaphore()
    for r in range(1, 16):
        pl.semaphore_signal(barrier, inc=1, device_id={"seq": (seq + r) % 16}, device_id_type=MESH_ID)
    for r in range(1, 8):
        pl.semaphore_signal(barrier, inc=1, device_id={"head": (head + r) % 8}, device_id_type=MESH_ID)

    first = (xi, yi)
    second = (yi, xi)

    def at(half, f, s):
        return s * SIDE + f if half == 0 else f * SIDE + s

    def send(src, dst, s_sem, r_sem, device):
        copy = pltpu.make_async_remote_copy(
            src_ref=src, dst_ref=dst, send_sem=s_sem, recv_sem=r_sem, device_id=device, device_id_type=MESH_ID
        )
        copy.start()
        return copy

    rate_c = column(rate[...], LOCAL_HEADS)
    upto = (iota((BLOCK, BLOCK), 0) <= iota((BLOCK, BLOCK), 1)).astype(F32)
    same = (iota((BLOCK, BLOCK), 0) // SEG) == (iota((BLOCK, BLOCK), 1) // SEG)
    upto_seg = jnp.where(same, upto, 0.0)
    p_dt = pdt[...]
    running = jnp.dot(p_dt * (-rate_c), upto, precision=HIGH, preferred_element_type=F32)
    total = running[:, BLOCK - 1 :]
    tails = jnp.exp(total - running) * p_dt
    b_dt = bdt[...]
    cum = jnp.dot(b_dt * (-rate_c), upto_seg, precision=HIGH, preferred_element_type=F32)
    lift = jnp.exp(cum)
    einv = jnp.exp(-cum) * b_dt

    stack = jnp.concatenate(
        [*split(tails), *split(lift), *split(einv), jnp.zeros((32, BLOCK), F32)], axis=0
    )
    stack_t = stack.T.astype(BF16)
    spread32 = ((iota((32, CH), 0) & 15) == (iota((32, CH), 1) >> 6)).astype(BF16)
    spread16 = ((iota((16, CH), 0)) == (iota((16, CH), 1) >> 6)).astype(F32)
    te = mm(stack_t[:, 0:32], spread32)
    tail_e[...] = te
    xw = (px[...].astype(F32) * te).astype(BF16)
    pb_t = pb[...].astype(F32).T.astype(BF16)
    for half in range(2):
        for c in range(NCH):
            lo = half * HALF + c * CW
            ug[half, c, first[half]] = mm(pb_t, xw[:, lo : lo + CW]).astype(BF16)

    sub = iota((8, 128), 0)
    lane = iota((8, 128), 1)
    eye16 = iota((16, 128), 0) == iota((16, 128), 1)
    total_row = jnp.sum(jnp.where(eye16, jnp.broadcast_to(total, (16, 128)), 0.0), axis=0, keepdims=True)
    tile0 = jnp.where(sub == 0, jnp.broadcast_to(total_row, (8, 128)), 0.0)
    for b in range(NB):
        tile0 = jnp.where(sub == 4 + b, par[b].astype(F32), tile0)
    table = (sub == jnp.broadcast_to(gid[...], (8, 128))).astype(F32)
    returns = ret[...]
    g_count = jnp.sum(table, axis=1, keepdims=True)
    g_sum = jnp.sum(table * returns, axis=1, keepdims=True)
    g_sq = jnp.sum(table * (returns * returns), axis=1, keepdims=True)
    tile1 = jnp.where(lane == 0, g_count, jnp.where(lane == 1, g_sum, jnp.where(lane == 2, g_sq, 0.0)))
    pk[seq, 0] = tile0
    pk[seq, 1] = tile1
    c_own = bc[...]
    for half in range(2):
        cg[half, second[half]] = c_own

    pl.semaphore_wait(barrier, 22)

    sent = []
    pk_in, c_in, u_in = [], [[], []], [[], []]
    for r in range(1, 16):
        copy = send(pk.at[seq], pk.at[seq], pk_s.at[r], pk_r.at[r], {"seq": (seq + r) % 16})
        pk_in.append(copy)
    sent += pk_in
    ORDER = (1, 3, 2)
    for half in range(2):
        s = second[half]
        for r in ORDER:
            peer = at(half, first[half], (s + r) % SIDE)
            c_in[half].append(
                send(cg.at[half, s], cg.at[half, s], c_s.at[half, r], c_r.at[half, r], {"seq": peer})
            )
    for c in range(NCH):
        for half in range(2):
            f = first[half]
            copies = {}
            for r in ORDER:
                peer = at(half, (f + r) % SIDE, second[half])
                copies[r] = send(
                    ug.at[half, c, f], ug.at[half, c, f], u_s.at[half, c, r], u_r.at[half, c, r], {"seq": peer}
                )
            u_in[half].append(copies)

    lift_e[...] = mm(stack_t[:, 32:64], spread32)
    einv_e[...] = mm(stack_t[:, 64:96], spread32)
    skip_e = jnp.sum(column(skip[...], LOCAL_HEADS) * spread16, axis=0, keepdims=True)
    gain_e = gain[...]
    scores = lax.dot_general(c_own, bb[...], (((1,), (1,)), ((), ())), preferred_element_type=F32)
    lower = upto_seg.T
    scores = (scores * lower).astype(BF16)
    smat[...] = scores
    x_own = bx[...].astype(F32)
    inner = mm(scores, (x_own * einv_e[...]).astype(BF16))
    y_s[...] = inner * lift_e[...] + skip_e * x_own
    z = bz[...].astype(F32)
    sz_s[...] = z / (1.0 + jnp.exp(-z))

    for copy in pk_in:
        copy.wait_recv()
    totals = pk[:, 0, 0, :]
    low16 = (iota((16, 16), 0) >= iota((16, 16), 1)).astype(F32)
    t_cum = jnp.dot(low16, totals, precision=HIGH, preferred_element_type=F32)
    t_e = jnp.dot(t_cum[:, :16], spread16, precision=HIGH, preferred_element_type=F32)
    for half in range(2):
        f0, s0 = first[half], second[half]
        parent = jnp.concatenate([pk[at(half, f0, s), 0, 4:8, :] for s in range(SIDE)], axis=0)
        onehot = (parent == iota((16, 128), 1).astype(F32)).astype(F32)
        lo = half * HALF
        t_half = t_e[:, lo : lo + HALF]
        t_par = jnp.dot(onehot[:, :16], t_half, precision=HIGH, preferred_element_type=F32)
        p_col = parent[:, 0:1]
        for f in range(SIDE):
            j = at(half, f, s0)
            pick = (iota((16, HALF), 0) == j).astype(F32)
            t_j = jnp.sum(t_half * pick, axis=0, keepdims=True)
            w = jnp.where(p_col >= j.astype(F32), jnp.exp(jnp.minimum(t_par - t_j, 0.0)), 0.0)
            for s in range(SIDE):
                wt[half, f, s, 0:4] = w[4 * s : 4 * s + 4]
    stats = pk[0, 1]
    for k in range(1, 16):
        stats = stats + pk[k, 1]
    floor_count = jnp.maximum(stats[:, 0:1], 1.0)
    mean = stats[:, 1:2] / floor_count
    spread = jnp.sqrt(stats[:, 2:3] / floor_count - mean * mean + 1.0)
    mean_row = jnp.sum(table * mean, axis=0, keepdims=True)
    spread_row = jnp.sum(table * spread, axis=0, keepdims=True)
    adv_row = (returns - mean_row) / spread_row

    for half in range(2):
        for copy in c_in[half]:
            copy.wait_recv()
    y_in = [[], []]
    for c in range(NCH):
        for half in range(2):
            f0, s0 = first[half], second[half]
            cs = slice(c * CW, (c + 1) * CW)
            for n, r in enumerate((0, 1, 3, 2)):
                f = (f0 + r) % SIDE
                if r:
                    u_in[half][c][(SIDE - r) % SIDE].wait_recv()
                u = ug[half, c, f]
                copies = {}
                for q in (2, 1, 3, 0):
                    s = (s0 + q) % SIDE
                    w = rows_to_tokens(wt[half, f, s, :, cs], CW)
                    part = mm(cg[half, s], u) * w
                    if n:
                        part = part + acc[q]
                    if n < 3:
                        acc[q] = part
                    elif q:
                        yp[half, c, q] = part.astype(BF16)
                        copies[q] = send(
                            yp.at[half, c, q],
                            yr.at[half, c, q],
                            y_ss.at[half, c, q],
                            y_rs.at[half, c, q],
                            {"seq": at(half, f0, s)},
                        )
                    else:
                        lo = half * HALF + c * CW
                        y_s[:, lo : lo + CW] = y_s[:, lo : lo + CW] + part * lift_e[:, lo : lo + CW]
            y_in[half].append(copies)

    for half in range(2):
        for s in range(SIDE):
            ct[half, s] = cg[half, s].astype(F32).T.astype(BF16)

    sq = jnp.zeros((BLOCK, 128), F32)
    al = jnp.zeros((BLOCK, 128), F32)
    for c in range(NCH):
        for half in range(2):
            lo = half * HALF + c * CW
            ws = slice(lo, lo + CW)
            got = None
            for q in (1, 3, 2):
                y_in[half][c][q].wait_recv()
                v = yr[half, c, q].astype(F32)
                got = v if got is None else got + v
            gated = (y_s[:, ws] + got * lift_e[:, ws]) * sz_s[:, ws]
            gated_s[:, ws] = gated
            squares = gated * gated
            inner = og[:, ws].astype(F32) * gain_e[:, ws] * gated
            for k in range(CW // 128):
                sq = sq + squares[:, 128 * k : 128 * k + 128]
                al = al + inner[:, 128 * k : 128 * k + 128]
    sq_row = jnp.sum(sq.T, axis=0, keepdims=True)
    al_row = jnp.sum(al.T, axis=0, keepdims=True)
    ar[head] = jnp.where(sub == 0, sq_row, jnp.where(sub == 1, al_row, 0.0))
    ar_in = [
        send(ar.at[head], ar.at[head], ar_s.at[r], ar_r.at[r], {"head": (head + r) % 8}) for r in (4, 3, 5, 2, 6, 7, 1)
    ]
    for copy in ar_in:
        copy.wait_recv()
    sums = ar[0]
    for k in range(1, 8):
        sums = sums + ar[k]
    scale = lax.rsqrt(sums[0:1] / (HEADS * HEAD_DIM) + EPSILON)
    along = adv_row * sums[1:2]
    kappa = scale * scale * scale * along / (HEADS * HEAD_DIM)
    sub128 = iota((128, 128), 0)
    rows = jnp.where(sub128 == 0, scale, jnp.where(sub128 == 1, scale * adv_row, jnp.where(sub128 == 2, kappa, 0.0)))
    cols = rows.T
    scale_c, push_c, kappa_c = cols[:, 0:1], cols[:, 1:2], cols[:, 2:3]

    d_in = [[], []]
    for c in range(NCH):
        for half in range(2):
            lo = half * HALF + c * CW
            ws = slice(lo, lo + CW)
            dy = (push_c * (og[:, ws].astype(F32) * gain_e[:, ws]) - kappa_c * gated_s[:, ws]) * sz_s[:, ws]
            dy_s[:, ws] = dy
            f0, s0 = first[half], second[half]
            dg[half, c, s0] = (dy * lift_e[:, ws]).astype(BF16)
            copies = {}
            for r in ORDER:
                copies[r] = send(
                    dg.at[half, c, s0],
                    dg.at[half, c, s0],
                    d_s.at[half, c, r],
                    d_r.at[half, c, r],
                    {"seq": at(half, f0, (s0 + r) % SIDE)},
                )
            d_in[half].append(copies)

    scores_t = smat[...].astype(F32).T.astype(BF16)
    for c in range(NCH):
        for half in range(2):
            lo = half * HALF + c * CW
            ws = slice(lo, lo + CW)
            back = mm(scores_t, dg[half, c, second[half]]) * einv_e[:, ws] + skip_e[:, ws] * dy_s[:, ws]
            grad_o[:, ws] = back.astype(BF16)
    out_o[...] = (gated_s[...] * scale_c * gain_e).astype(BF16)

    g_in = [[], []]
    for c in range(NCH):
        for half in range(2):
            f0, s0 = first[half], second[half]
            cs = slice(c * CW, (c + 1) * CW)
            for n, r in enumerate((0, 1, 3, 2)):
                s = (s0 + r) % SIDE
                if r:
                    d_in[half][c][(SIDE - r) % SIDE].wait_recv()
                d = dg[half, c, s].astype(F32)
                copies = {}
                for q in (2, 1, 3, 0):
                    f = (f0 + q) % SIDE
                    w = rows_to_tokens(wt[half, f, s, :, cs], CW)
                    part = mm(ct[half, s], (d * w).astype(BF16))
                    if n:
                        part = part + acc[q]
                    if n < 3 or q == 0:
                        acc[q if n < 3 else 4 + half * NCH + c] = part
                    else:
                        gp[half, c, q] = part.astype(BF16)
                        copies[q] = send(
                            gp.at[half, c, q],
                            gr.at[half, c, q],
                            g_s.at[half, c, q],
                            g_r.at[half, c, q],
                            {"seq": at(half, f, s0)},
                        )
            g_in[half].append(copies)

    p_b = pb[...]
    for c in range(NCH):
        for half in range(2):
            lo = half * HALF + c * CW
            ws = slice(lo, lo + CW)
            g = acc[4 + half * NCH + c]
            for q in (1, 3, 2):
                g_in[half][c][q].wait_recv()
                g = g + gr[half, c, q].astype(F32)
            prompt_o[:, ws] = mm(p_b, g.astype(BF16)) * tail_e[:, ws]

    for copy in sent + ar_in:
        copy.wait_send()
    for half in range(2):
        for copy in c_in[half]:
            copy.wait_send()
        for group in (u_in, y_in, d_in, g_in):
            for copies in group[half]:
                for copy in copies.values():
                    copy.wait_send()


def local(
    prompt_x, prompt_b, prompt_dt, branch_x, branch_b, branch_c, branch_z, branch_dt,
    a_rate, d_skip, norm_gain, branch_parent, group_ids, returns, out_grad,
):
    vm = pl.BlockSpec(memory_space=pltpu.VMEM)
    sm = pl.BlockSpec(memory_space=pltpu.SMEM)
    dma = pltpu.SemaphoreType.DMA
    V = pltpu.VMEM
    return pl.pallas_call(
        kernel,
        out_shape=(
            jax.ShapeDtypeStruct((BLOCK, CH), BF16),
            jax.ShapeDtypeStruct((BLOCK, CH), BF16),
            jax.ShapeDtypeStruct((BLOCK, CH), F32),
        ),
        in_specs=[vm] * 11 + [sm] + [vm] * 3,
        out_specs=(vm, vm, vm),
        scratch_shapes=[
            V((16, 2, 8, 128), F32),
            V((8, 8, 128), F32),
            V((2, NCH, SIDE, STATE, CW), BF16),
            V((2, SIDE, BLOCK, STATE), BF16),
            V((2, SIDE, STATE, BLOCK), BF16),
            V((2, NCH, SIDE, BLOCK, CW), BF16),
            V((2, NCH, SIDE, BLOCK, CW), BF16),
            V((2, NCH, SIDE, BLOCK, CW), BF16),
            V((2, NCH, SIDE, STATE, CW), BF16),
            V((2, NCH, SIDE, STATE, CW), BF16),
            V((4 + 2 * NCH, BLOCK, CW), F32),
            V((2, SIDE, SIDE, 8, HALF), F32),
            V((BLOCK, CH), F32),
            V((BLOCK, CH), F32),
            V((BLOCK, CH), F32),
            V((BLOCK, BLOCK), BF16),
            V((BLOCK, CH), F32),
            V((BLOCK, CH), F32),
            V((BLOCK, CH), F32),
            V((BLOCK, CH), F32),
            dma((16,)), dma((16,)), dma((8,)), dma((8,)),
            dma((2, NCH, SIDE)), dma((2, NCH, SIDE)),
            dma((2, SIDE)), dma((2, SIDE)),
            dma((2, NCH, SIDE)), dma((2, NCH, SIDE)),
            dma((2, NCH, SIDE)), dma((2, NCH, SIDE)),
            dma((2, NCH, SIDE)), dma((2, NCH, SIDE)),
        ],
        compiler_params=pltpu.CompilerParams(
            collective_id=0, has_side_effects=True, vmem_limit_bytes=40 * 2**20
        ),
    )(
        prompt_x, prompt_b, prompt_dt, branch_x, branch_b, branch_c, branch_z, branch_dt,
        a_rate.reshape(1, -1), d_skip.reshape(1, -1), norm_gain.reshape(1, -1), branch_parent,
        group_ids.reshape(1, -1), returns.reshape(1, -1), out_grad,
    )


def solution(mesh):
    rows = P(("parts", "seq"), "head")
    steps = P("head", ("parts", "seq"))
    heads = P("head")
    tokens = P(("parts", "seq"))
    return jax.shard_map(
        local,
        mesh=mesh,
        in_specs=(
            rows, rows, steps, rows, rows, rows, rows, steps,
            heads, heads, heads, tokens, tokens, tokens, rows,
        ),
        out_specs=(rows, rows, rows),
        check_vma=False,
    )
```

time: 420 us -> 60.3 us (0.14)
  waiting for transfers between devices: 242 us -> 0 us
  blocking collectives: 55.8 us -> 0 us
  Pallas kernels: 0 us -> 46.7 us
  other arithmetic: 46 us -> 0 us
  matrix products: 35.3 us -> 0 us
  between operations: 14.8 us -> 0.68 us
  local copies, waits for them, and re-layouts: 21.6 us -> 12.3 us
    all_gather x3 -> x0, waiting for transfers between devices: 160 us -> none  [the longest x2 94.2 us: prefix(): pieces = jax.tree.map(lambda part: lax.all_gather(part, axis), value)]
    unnamed x5 -> x0, waiting for transfers between devices: 82.3 us -> none
    pallas_call x0 -> x1, Pallas kernels: none -> 46.7 us  [local(): pl.pallas_call(kernel, out_shape=(jax.ShapeDtypeStruct((BLOCK, CH), BF16)...]
    unnamed x1 -> x0, blocking collectives: 41 us -> none
    dot_general x13 -> x0, matrix products: 35.3 us -> none  [the longest x1 11 us: local(): jnp.einsum('bm,mhpn->bhpn', chosen, piece, precision=PRECISE)]
    select_n x30 -> x0, other arithmetic: 35.3 us -> none  [turn(): jnp.where(position < mine, new, old)]
    psum x1 -> x0, blocking collectives: 14.8 us -> none  [local(): total_sq = lax.psum(jnp.sum(gated * gated, axis=1), 'head')]
    unnamed x43 -> x33, local copies, waits for them, and re-layouts: 3.73 us -> 12.3 us
  transfers between devices with their start and end apart: 4 -> 0, of which waited for: 4 -> 0; matrix products, arithmetic and copies ran while one was open for 3% -> 0% of each run, Pallas kernels for 0% -> 0%
where the time goes in v1:
time: 60.3 us; the launch traced here: 59.7 us
  Pallas kernels  46.7 us (77%)
  local copies, waits for them, and re-layouts  12.3 us (20%)
  between operations  0.68 us (1%)
    pallas_call x1, Pallas kernels, local(): pl.pallas_call(kernel, out_shape=(jax.ShapeDtypeStruct((BLOCK, CH), BF16)...  46.7 us
    unnamed x33, local copies, waits for them, and re-layouts  12.3 us

profile of v1, /device:TPU:0, one launch (start us, length us, event | category | flops | bytes accessed | tf_op | source)
XLA Modules:
  0.0 59.7 jit_solution(4083232240025932722)
XLA Ops:
  0.6 0.0 copy-start.7
  0.6 0.0 copy-start.10
  0.7 0.0 copy-start.11
  0.7 0.7 %copy-done.7 = f32[16,128]{1,0:T(8,128)S(1)} copy-done((f32[16,128]{1,0:T(8,128)S(1)}, f32[16,128]{1,0:T(8,128)}, u32[]{:S(2)}) %copy-start.7) | copy-done | bytes 8216
  1.3 0.0 copy-done.10
  1.3 0.0 copy-done.11
  1.3 0.0 copy-start
  1.3 0.9 %copy-done = bf16[128,1024]{1,0:T(8,128)(2,1)S(1)} copy-done((bf16[128,1024]{1,0:T(8,128)(2,1)S(1)}, bf16[128,1024]{1,0:T(8,128)(2,1)}, u32[]{:S(2)}) %copy-start) | copy-done | bytes 262168
  2.3 0.0 copy-start.1
  2.3 0.9 %copy-done.1 = bf16[128,1024]{1,0:T(8,128)(2,1)S(1)} copy-done((bf16[128,1024]{1,0:T(8,128)(2,1)S(1)}, bf16[128,1024]{1,0:T(8,128)(2,1)}, u32[]{:S(2)}) %copy-start.1) | copy-done | bytes 262168
  3.2 0.0 copy-start.2
  3.2 0.9 %copy-done.2 = bf16[128,1024]{1,0:T(8,128)(2,1)S(1)} copy-done((bf16[128,1024]{1,0:T(8,128)(2,1)S(1)}, bf16[128,1024]{1,0:T(8,128)(2,1)}, u32[]{:S(2)}) %copy-start.2) | copy-done | bytes 262168
  4.2 0.0 copy-start.3
  4.2 0.9 %copy-done.3 = bf16[128,1024]{1,0:T(8,128)(2,1)S(1)} copy-done((bf16[128,1024]{1,0:T(8,128)(2,1)S(1)}, bf16[128,1024]{1,0:T(8,128)(2,1)}, u32[]{:S(2)}) %copy-start.3) | copy-done | bytes 262168
  5.1 0.0 copy-start.4
  5.1 0.8 %copy-done.4 = bf16[128,128]{1,0:T(8,128)(2,1)S(1)} copy-done((bf16[128,128]{1,0:T(8,128)(2,1)S(1)}, bf16[128,128]{1,0:T(8,128)(2,1)}, u32[]{:S(2)}) %copy-start.4) | copy-done | bytes 32792
  5.9 0.0 copy-start.5
  5.9 0.8 %copy-done.5 = bf16[128,128]{1,0:T(8,128)(2,1)S(1)} copy-done((bf16[128,128]{1,0:T(8,128)(2,1)S(1)}, bf16[128,128]{1,0:T(8,128)(2,1)}, u32[]{:S(2)}) %copy-start.5) | copy-done | bytes 32792
  6.7 0.0 copy-start.6
  6.7 0.8 %copy-done.6 = bf16[128,128]{1,0:T(8,128)(2,1)S(1)} copy-done((bf16[128,128]{1,0:T(8,128)(2,1)S(1)}, bf16[128,128]{1,0:T(8,128)(2,1)}, u32[]{:S(2)}) %copy-start.6) | copy-done | bytes 32792
  7.4 0.0 copy-start.8
  7.4 0.7 %copy-done.8 = f32[16,128]{1,0:T(8,128)S(1)} copy-done((f32[16,128]{1,0:T(8,128)S(1)}, f32[16,128]{1,0:T(8,128)}, u32[]{:S(2)}) %copy-start.8) | copy-done | bytes 8216
  8.1 0.0 copy-start.9
  8.1 0.7 %copy-done.9 = f32[1024]{0:T(1024)S(1)} copy-done((f32[1024]{0:T(1024)S(1)}, f32[1024]{0:T(1024)}, u32[]{:S(2)}) %copy-start.9) | copy-done | bytes 4120
  8.8 0.0 copy-start.12
  8.8 0.7 %copy-done.12 = s32[4]{0:T(128)S(1)} copy-done((s32[4]{0:T(128)S(1)}, s32[4]{0:T(128)}, u32[]{:S(2)}) %copy-start.12) | copy-done | bytes 40
  9.5 0.0 copy-start.13
  9.5 0.7 %copy-done.13 = s32[128]{0:T(128)S(1)} copy-done((s32[128]{0:T(128)S(1)}, s32[128]{0:T(128)}, u32[]{:S(2)}) %copy-start.13) | copy-done | bytes 536
  10.1 0.0 copy-start.14
  10.1 0.7 %copy-done.14 = f32[128]{0:T(128)S(1)} copy-done((f32[128]{0:T(128)S(1)}, f32[128]{0:T(128)}, u32[]{:S(2)}) %copy-start.14) | copy-done | bytes 536
  10.8 46.7 %shard_map.166 = (bf16[128,1024]{1,0:T(8,128)(2,1)S(1)}, bf16[128,1024]{1,0:T(8,128)(2,1)S(1)}, f32[128,1024]{1,0:T(8,128)S(1)}) custom-call(bf16[128,1024]{1,0:T(8,128)(2,1)S(1)} %copy-done, bf16[128,128]{1,0:T(8,128)(2,1)S(1)} %copy-done.4, f32[16,128]{1,0:T(8,128)S(1)} %copy-done.7, bf16[128,1024]{1,0:T(8,128)(2,1)S(1)} %copy-done.1, ...), custom_call_target="tpu_custom_call" | custom-call | tf_op jit(solution)/shard_map/pallas_call | solution.py:365
  57.5 0.7 %copy.21 = bf16[128,1024]{1,0:T(8,128)(2,1)} copy(bf16[128,1024]{1,0:T(8,128)(2,1)S(1)} %get-tuple-element.6) | data formatting | bytes 524288
  58.2 0.7 %copy.22 = bf16[128,1024]{1,0:T(8,128)(2,1)} copy(bf16[128,1024]{1,0:T(8,128)(2,1)S(1)} %get-tuple-element.7) | data formatting | bytes 524288
  58.9 0.8 %copy.23 = f32[128,1024]{1,0:T(8,128)} copy(f32[128,1024]{1,0:T(8,128)S(1)} %get-tuple-element.8) | data formatting | bytes 1048576
Async XLA Ops:
  0.6 0.7 %copy-start.7 = (f32[16,128]{1,0:T(8,128)S(1)}, f32[16,128]{1,0:T(8,128)}, u32[]{:S(2)}) copy-start(f32[16,128]{1,0:T(8,128)} %pdt.1) | copy-start | bytes 24580
  0.6 0.7 %copy-start.10 = (f32[16]{0:T(128)S(1)}, f32[16]{0:T(128)}, u32[]{:S(2)}) copy-start(f32[16]{0:T(128)} %param.23) | copy-start | bytes 196
  0.7 0.7 %copy-start.11 = (f32[16]{0:T(128)S(1)}, f32[16]{0:T(128)}, u32[]{:S(2)}) copy-start(f32[16]{0:T(128)} %param.24) | copy-start | bytes 196
  1.3 1.0 %copy-start = (bf16[128,1024]{1,0:T(8,128)(2,1)S(1)}, bf16[128,1024]{1,0:T(8,128)(2,1)}, u32[]{:S(2)}) copy-start(bf16[128,1024]{1,0:T(8,128)(2,1)} %px.1) | copy-start | bytes 786436
  2.3 0.9 %copy-start.1 = (bf16[128,1024]{1,0:T(8,128)(2,1)S(1)}, bf16[128,1024]{1,0:T(8,128)(2,1)}, u32[]{:S(2)}) copy-start(bf16[128,1024]{1,0:T(8,128)(2,1)} %bx.1) | copy-start | bytes 786436
  3.2 0.9 %copy-start.2 = (bf16[128,1024]{1,0:T(8,128)(2,1)S(1)}, bf16[128,1024]{1,0:T(8,128)(2,1)}, u32[]{:S(2)}) copy-start(bf16[128,1024]{1,0:T(8,128)(2,1)} %bz.1) | copy-start | bytes 786436
  4.2 0.9 %copy-start.3 = (bf16[128,1024]{1,0:T(8,128)(2,1)S(1)}, bf16[128,1024]{1,0:T(8,128)(2,1)}, u32[]{:S(2)}) copy-start(bf16[128,1024]{1,0:T(8,128)(2,1)} %og.1) | copy-start | bytes 786436
  5.1 0.8 %copy-start.4 = (bf16[128,128]{1,0:T(8,128)(2,1)S(1)}, bf16[128,128]{1,0:T(8,128)(2,1)}, u32[]{:S(2)}) copy-start(bf16[128,128]{1,0:T(8,128)(2,1)} %pb.1) | copy-start | bytes 98308
  5.9 0.8 %copy-start.5 = (bf16[128,128]{1,0:T(8,128)(2,1)S(1)}, bf16[128,128]{1,0:T(8,128)(2,1)}, u32[]{:S(2)}) copy-start(bf16[128,128]{1,0:T(8,128)(2,1)} %bb.1) | copy-start | bytes 98308
  6.7 0.8 %copy-start.6 = (bf16[128,128]{1,0:T(8,128)(2,1)S(1)}, bf16[128,128]{1,0:T(8,128)(2,1)}, u32[]{:S(2)}) copy-start(bf16[128,128]{1,0:T(8,128)(2,1)} %bc.1) | copy-start | bytes 98308
  7.4 0.7 %copy-start.8 = (f32[16,128]{1,0:T(8,128)S(1)}, f32[16,128]{1,0:T(8,128)}, u32[]{:S(2)}) copy-start(f32[16,128]{1,0:T(8,128)} %bdt.1) | copy-start | bytes 24580
  8.1 0.7 %copy-start.9 = (f32[1024]{0:T(1024)S(1)}, f32[1024]{0:T(1024)}, u32[]{:S(2)}) copy-start(f32[1024]{0:T(1024)} %param.25) | copy-start | bytes 12292
  8.8 0.7 %copy-start.12 = (s32[4]{0:T(128)S(1)}, s32[4]{0:T(128)}, u32[]{:S(2)}) copy-start(s32[4]{0:T(128)} %par.1) | copy-start | bytes 52
  9.5 0.7 %copy-start.13 = (s32[128]{0:T(128)S(1)}, s32[128]{0:T(128)}, u32[]{:S(2)}) copy-start(s32[128]{0:T(128)} %param.27) | copy-start | bytes 1540
  10.1 0.7 %copy-start.14 = (f32[128]{0:T(128)S(1)}, f32[128]{0:T(128)}, u32[]{:S(2)}) copy-start(f32[128]{0:T(128)} %param.28) | copy-start | bytes 1540

commit v2 on v1

--- a/solution.py
+++ b/solution.py
@@ -49,8 +49,9 @@
 
 
 def kernel(
-    px, pb, pdt, bx, bb, bc, bz, bdt, rate, skip, gain, par, gid, ret, og,
+    px_h, pb_h, pdt_h, bx_h, bb_h, bc_h, bz_h, bdt_h, rate_h, skip_h, gain_h, par_h, gid_h, ret_h, og_h,
     out_o, grad_o, prompt_o,
+    px, pb, pdt, bx, bb, bc, bz, bdt, rate, skip, gain, par, gid, ret, og, in_sem,
     pk, ar, ug, cg, ct, yp, yr, dg, gp, gr, acc, wt, tail_e, lift_e, einv_e, smat, y_s, gated_s, sz_s, dy_s,
     pk_s, pk_r, ar_s, ar_r, u_s, u_r, c_s, c_r, y_ss, y_rs, d_s, d_r, g_s, g_r,
 ):
@@ -58,6 +59,19 @@
     head = lax.axis_index("head")
     yi, xi = seq // SIDE, seq % SIDE
 
+    loads = {}
+    for n, (name, src, dst) in enumerate((
+        ("pdt", pdt_h, pdt), ("rate", rate_h, rate), ("px", px_h, px), ("pb", pb_h, pb), ("bdt", bdt_h, bdt),
+        ("par", par_h, par), ("gid", gid_h, gid), ("ret", ret_h, ret), ("bc", bc_h, bc), ("skip", skip_h, skip),
+        ("bb", bb_h, bb), ("bx", bx_h, bx), ("bz", bz_h, bz), ("gain", gain_h, gain), ("og", og_h, og),
+    )):
+        loads[name] = pltpu.make_async_copy(src, dst, in_sem.at[n])
+        loads[name].start()
+
+    def loaded(*names):
+        for name in names:
+            loads[name].wait()
+
     barrier = pltpu.get_barrier_semaphore()
     for r in range(1, 16):
         pl.semaphore_signal(barrier, inc=1, device_id={"seq": (seq + r) % 16}, device_id_type=MESH_ID)
@@ -75,8 +89,15 @@
             src_ref=src, dst_ref=dst, send_sem=s_sem, recv_sem=r_sem, device_id=device, device_id_type=MESH_ID
         )
         copy.start()
+        sent.append(copy)
         return copy
 
+    sent = []
+
+    def arrive(copy):
+        copy.wait_recv()
+
+    loaded("pdt", "rate", "bdt")
     rate_c = column(rate[...], LOCAL_HEADS)
     upto = (iota((BLOCK, BLOCK), 0) <= iota((BLOCK, BLOCK), 1)).astype(F32)
     same = (iota((BLOCK, BLOCK), 0) // SEG) == (iota((BLOCK, BLOCK), 1) // SEG)
@@ -98,6 +119,7 @@
     spread16 = ((iota((16, CH), 0)) == (iota((16, CH), 1) >> 6)).astype(F32)
     te = mm(stack_t[:, 0:32], spread32)
     tail_e[...] = te
+    loaded("px", "pb")
     xw = (px[...].astype(F32) * te).astype(BF16)
     pb_t = pb[...].astype(F32).T.astype(BF16)
     for half in range(2):
@@ -105,6 +127,7 @@
             lo = half * HALF + c * CW
             ug[half, c, first[half]] = mm(pb_t, xw[:, lo : lo + CW]).astype(BF16)
 
+    loaded("par", "gid", "ret", "bc")
     sub = iota((8, 128), 0)
     lane = iota((8, 128), 1)
     eye16 = iota((16, 128), 0) == iota((16, 128), 1)
@@ -126,12 +149,10 @@
 
     pl.semaphore_wait(barrier, 22)
 
-    sent = []
     pk_in, c_in, u_in = [], [[], []], [[], []]
     for r in range(1, 16):
         copy = send(pk.at[seq], pk.at[seq], pk_s.at[r], pk_r.at[r], {"seq": (seq + r) % 16})
         pk_in.append(copy)
-    sent += pk_in
     ORDER = (1, 3, 2)
     for half in range(2):
         s = second[half]
@@ -151,6 +172,7 @@
                 )
             u_in[half].append(copies)
 
+    loaded("skip", "bb", "bx", "bz", "gain", "og")
     lift_e[...] = mm(stack_t[:, 32:64], spread32)
     einv_e[...] = mm(stack_t[:, 64:96], spread32)
     skip_e = jnp.sum(column(skip[...], LOCAL_HEADS) * spread16, axis=0, keepdims=True)
@@ -166,7 +188,7 @@
     sz_s[...] = z / (1.0 + jnp.exp(-z))
 
     for copy in pk_in:
-        copy.wait_recv()
+        arrive(copy)
     totals = pk[:, 0, 0, :]
     low16 = (iota((16, 16), 0) >= iota((16, 16), 1)).astype(F32)
     t_cum = jnp.dot(low16, totals, precision=HIGH, preferred_element_type=F32)
@@ -198,7 +220,7 @@
 
     for half in range(2):
         for copy in c_in[half]:
-            copy.wait_recv()
+            arrive(copy)
     y_in = [[], []]
     for c in range(NCH):
         for half in range(2):
@@ -207,7 +229,7 @@
             for n, r in enumerate((0, 1, 3, 2)):
                 f = (f0 + r) % SIDE
                 if r:
-                    u_in[half][c][(SIDE - r) % SIDE].wait_recv()
+                    arrive(u_in[half][c][(SIDE - r) % SIDE])
                 u = ug[half, c, f]
                 copies = {}
                 for q in (2, 1, 3, 0):
@@ -244,7 +266,7 @@
             ws = slice(lo, lo + CW)
             got = None
             for q in (1, 3, 2):
-                y_in[half][c][q].wait_recv()
+                arrive(y_in[half][c][q])
                 v = yr[half, c, q].astype(F32)
                 got = v if got is None else got + v
             gated = (y_s[:, ws] + got * lift_e[:, ws]) * sz_s[:, ws]
@@ -261,7 +283,7 @@
         send(ar.at[head], ar.at[head], ar_s.at[r], ar_r.at[r], {"head": (head + r) % 8}) for r in (4, 3, 5, 2, 6, 7, 1)
     ]
     for copy in ar_in:
-        copy.wait_recv()
+        arrive(copy)
     sums = ar[0]
     for k in range(1, 8):
         sums = sums + ar[k]
@@ -310,7 +332,7 @@
             for n, r in enumerate((0, 1, 3, 2)):
                 s = (s0 + r) % SIDE
                 if r:
-                    d_in[half][c][(SIDE - r) % SIDE].wait_recv()
+                    arrive(d_in[half][c][(SIDE - r) % SIDE])
                 d = dg[half, c, s].astype(F32)
                 copies = {}
                 for q in (2, 1, 3, 0):
@@ -339,19 +361,21 @@
             ws = slice(lo, lo + CW)
             g = acc[4 + half * NCH + c]
             for q in (1, 3, 2):
-                g_in[half][c][q].wait_recv()
+                arrive(g_in[half][c][q])
                 g = g + gr[half, c, q].astype(F32)
             prompt_o[:, ws] = mm(p_b, g.astype(BF16)) * tail_e[:, ws]
 
-    for copy in sent + ar_in:
+    for copy in sent:
         copy.wait_send()
-    for half in range(2):
-        for copy in c_in[half]:
-            copy.wait_send()
-        for group in (u_in, y_in, d_in, g_in):
-            for copies in group[half]:
-                for copy in copies.values():
-                    copy.wait_send()
+
+
+PIECES = 4
+
+
+def hand_over(a, b, c, a_out, b_out, c_out):
+    a_out[...] = a[...]
+    b_out[...] = b[...]
+    c_out[...] = c[...]
 
 
 def local(
@@ -359,19 +383,25 @@
     a_rate, d_skip, norm_gain, branch_parent, group_ids, returns, out_grad,
 ):
     vm = pl.BlockSpec(memory_space=pltpu.VMEM)
-    sm = pl.BlockSpec(memory_space=pltpu.SMEM)
     dma = pltpu.SemaphoreType.DMA
     V = pltpu.VMEM
-    return pl.pallas_call(
+    results = pl.pallas_call(
         kernel,
         out_shape=(
             jax.ShapeDtypeStruct((BLOCK, CH), BF16),
             jax.ShapeDtypeStruct((BLOCK, CH), BF16),
             jax.ShapeDtypeStruct((BLOCK, CH), F32),
         ),
-        in_specs=[vm] * 11 + [sm] + [vm] * 3,
+        in_specs=[pl.BlockSpec(memory_space=pltpu.HBM)] * 15,
         out_specs=(vm, vm, vm),
         scratch_shapes=[
+            V((BLOCK, CH), BF16), V((BLOCK, STATE), BF16), V((LOCAL_HEADS, BLOCK), F32),
+            V((BLOCK, CH), BF16), V((BLOCK, STATE), BF16), V((BLOCK, STATE), BF16),
+            V((BLOCK, CH), BF16), V((LOCAL_HEADS, BLOCK), F32),
+            V((1, LOCAL_HEADS), F32), V((1, LOCAL_HEADS), F32), V((1, CH), F32),
+            pltpu.SMEM((NB,), jnp.int32), V((1, BLOCK), jnp.int32), V((1, BLOCK), F32),
+            V((BLOCK, CH), BF16),
+            dma((15,)),
             V((16, 2, 8, 128), F32),
             V((8, 8, 128), F32),
             V((2, NCH, SIDE, STATE, CW), BF16),
@@ -402,11 +432,19 @@
         compiler_params=pltpu.CompilerParams(
             collective_id=0, has_side_effects=True, vmem_limit_bytes=40 * 2**20
         ),
-    )(
+    )(*(pltpu.with_memory_space_constraint(v, pltpu.HBM) for v in (
         prompt_x, prompt_b, prompt_dt, branch_x, branch_b, branch_c, branch_z, branch_dt,
         a_rate.reshape(1, -1), d_skip.reshape(1, -1), norm_gain.reshape(1, -1), branch_parent,
         group_ids.reshape(1, -1), returns.reshape(1, -1), out_grad,
-    )
+    )))
+    hbm = pl.BlockSpec(memory_space=pltpu.HBM)
+    return pl.pallas_call(
+        hand_over,
+        out_shape=tuple(jax.ShapeDtypeStruct(r.shape, r.dtype) for r in results),
+        in_specs=[vm] * 3,
+        out_specs=(vm,) * 3,
+        compiler_params=pltpu.CompilerParams(vmem_limit_bytes=16 * 2**20),
+    )(*results)
 
 
 def solution(mesh):

time: 60.3 us -> 48.2 us (0.80)
  local copies, waits for them, and re-layouts: 12.3 us -> 0 us
  Pallas kernels: 46.7 us -> 47.4 us
    unnamed x33 -> x0, local copies, waits for them, and re-layouts: 12.3 us -> none
    pallas_call x0 -> x1, Pallas kernels: none -> 1.04 us  [local(): pl.pallas_call(hand_over, out_shape=tuple((jax.ShapeDtypeStruct(r.shape,...]
where the time goes in v2:
time: 48.2 us; the launch traced here: 48 us
  Pallas kernels  47.4 us (98%)
  between operations  0.64 us (1%)
    pallas_call x1, Pallas kernels, local(): pl.pallas_call(kernel, out_shape=(jax.ShapeDtypeStruct((BLOCK, CH), BF16)...  46.4 us
    pallas_call x1, Pallas kernels, local(): pl.pallas_call(hand_over, out_shape=tuple((jax.ShapeDtypeStruct(r.shape,...  1.04 us

profile of v2, /device:TPU:0, one launch (start us, length us, event | category | flops | bytes accessed | tf_op | source)
XLA Modules:
  0.0 48.0 jit_solution(9127583125951661156)
XLA Ops:
  0.6 46.4 %shard_map.166 = (bf16[128,1024]{1,0:T(8,128)(2,1)S(1)}, bf16[128,1024]{1,0:T(8,128)(2,1)S(1)}, f32[128,1024]{1,0:T(8,128)S(1)}) custom-call(bf16[128,1024]{1,0:T(8,128)(2,1)} %px_h.1, bf16[128,128]{1,0:T(8,128)(2,1)} %pb_h.1, f32[16,128]{1,0:T(8,128)} %pdt_h.1, bf16[128,1024]{1,0:T(8,128)(2,1)} %bx_h.1, bf16[128,128]{1,0:T(8,128)(2,1)} %bb_h.1, ...), custom_call_target="tpu_custom_call" | custom-call | tf_op jit(solution)/shard_map/pallas_call | solution.py:388
  47.0 1.0 %shard_map.167 = (bf16[128,1024]{1,0:T(8,128)(2,1)}, bf16[128,1024]{1,0:T(8,128)(2,1)}, f32[128,1024]{1,0:T(8,128)}) custom-call(bf16[128,1024]{1,0:T(8,128)(2,1)S(1)} %get-tuple-element.6.a, bf16[128,1024]{1,0:T(8,128)(2,1)S(1)} %get-tuple-element.7.b, f32[128,1024]{1,0:T(8,128)S(1)} %get-tuple-element.8.c), custom_call_target="tpu_custom_call" | custom-call | tf_op jit(solution)/shard_map/pallas_call | solution.py:441

commit v3 on v2

--- a/solution.py
+++ b/solution.py
@@ -52,7 +52,7 @@
     px_h, pb_h, pdt_h, bx_h, bb_h, bc_h, bz_h, bdt_h, rate_h, skip_h, gain_h, par_h, gid_h, ret_h, og_h,
     out_o, grad_o, prompt_o,
     px, pb, pdt, bx, bb, bc, bz, bdt, rate, skip, gain, par, gid, ret, og, in_sem,
-    pk, ar, ug, cg, ct, yp, yr, dg, gp, gr, acc, wt, tail_e, lift_e, einv_e, smat, y_s, gated_s, sz_s, dy_s,
+    pk, ar, ug, cg, ct, yp, yr, dg, gp, gr, acc, wt, tail_e, lift_e, einv_e, smat, y_s, gated_s, sz_s, dy_s, og_s,
     pk_s, pk_r, ar_s, ar_r, u_s, u_r, c_s, c_r, y_ss, y_rs, d_s, d_r, g_s, g_r,
 ):
     seq = lax.axis_index("seq")
@@ -73,8 +73,13 @@
             loads[name].wait()
 
     barrier = pltpu.get_barrier_semaphore()
-    for r in range(1, 16):
-        pl.semaphore_signal(barrier, inc=1, device_id={"seq": (seq + r) % 16}, device_id_type=MESH_ID)
+    for r in range(1, SIDE):
+        pl.semaphore_signal(
+            barrier, inc=1, device_id={"seq": yi * SIDE + (xi + r) % SIDE}, device_id_type=MESH_ID
+        )
+        pl.semaphore_signal(
+            barrier, inc=1, device_id={"seq": (yi + r) % SIDE * SIDE + xi}, device_id_type=MESH_ID
+        )
     for r in range(1, 8):
         pl.semaphore_signal(barrier, inc=1, device_id={"head": (head + r) % 8}, device_id_type=MESH_ID)
 
@@ -132,27 +137,29 @@
     lane = iota((8, 128), 1)
     eye16 = iota((16, 128), 0) == iota((16, 128), 1)
     total_row = jnp.sum(jnp.where(eye16, jnp.broadcast_to(total, (16, 128)), 0.0), axis=0, keepdims=True)
-    tile0 = jnp.where(sub == 0, jnp.broadcast_to(total_row, (8, 128)), 0.0)
+    parents = jnp.zeros((8, 128), F32)
     for b in range(NB):
-        tile0 = jnp.where(sub == 4 + b, par[b].astype(F32), tile0)
+        parents = jnp.where(sub == 4 + b, par[b].astype(F32), parents)
     table = (sub == jnp.broadcast_to(gid[...], (8, 128))).astype(F32)
     returns = ret[...]
     g_count = jnp.sum(table, axis=1, keepdims=True)
     g_sum = jnp.sum(table * returns, axis=1, keepdims=True)
     g_sq = jnp.sum(table * (returns * returns), axis=1, keepdims=True)
-    tile1 = jnp.where(lane == 0, g_count, jnp.where(lane == 1, g_sum, jnp.where(lane == 2, g_sq, 0.0)))
-    pk[seq, 0] = tile0
-    pk[seq, 1] = tile1
+    tile = jnp.where(sub == 0, jnp.broadcast_to(total_row, (8, 128)), 0.0)
+    tile = jnp.where((lane >= 32) & (lane < 48), parents, tile)
+    for n, value in enumerate((g_count, g_sum, g_sq)):
+        tile = jnp.where(lane == 64 + n, value, tile)
+    pk[yi, xi] = tile
     c_own = bc[...]
     for half in range(2):
         cg[half, second[half]] = c_own
 
-    pl.semaphore_wait(barrier, 22)
+    pl.semaphore_wait(barrier, 13)
 
     pk_in, c_in, u_in = [], [[], []], [[], []]
-    for r in range(1, 16):
-        copy = send(pk.at[seq], pk.at[seq], pk_s.at[r], pk_r.at[r], {"seq": (seq + r) % 16})
-        pk_in.append(copy)
+    for r in (2, 1, 3):
+        peer = yi * SIDE + (xi + r) % SIDE
+        pk_in.append(send(pk.at[yi, xi], pk.at[yi, xi], pk_s.at[0, r], pk_r.at[0, r], {"seq": peer}))
     ORDER = (1, 3, 2)
     for half in range(2):
         s = second[half]
@@ -161,16 +168,19 @@
             c_in[half].append(
                 send(cg.at[half, s], cg.at[half, s], c_s.at[half, r], c_r.at[half, r], {"seq": peer})
             )
-    for c in range(NCH):
+    def send_updates(c, distances):
         for half in range(2):
             f = first[half]
-            copies = {}
-            for r in ORDER:
+            if len(u_in[half]) == c:
+                u_in[half].append({})
+            copies = u_in[half][c]
+            for r in distances:
                 peer = at(half, (f + r) % SIDE, second[half])
                 copies[r] = send(
                     ug.at[half, c, f], ug.at[half, c, f], u_s.at[half, c, r], u_r.at[half, c, r], {"seq": peer}
                 )
-            u_in[half].append(copies)
+
+    send_updates(0, (1, 3))
 
     loaded("skip", "bb", "bx", "bz", "gain", "og")
     lift_e[...] = mm(stack_t[:, 32:64], spread32)
@@ -189,18 +199,29 @@
 
     for copy in pk_in:
         arrive(copy)
-    totals = pk[:, 0, 0, :]
+    pk_in = []
+    for r in (2, 1, 3):
+        peer = (yi + r) % SIDE * SIDE + xi
+        pk_in.append(send(pk.at[yi], pk.at[yi], pk_s.at[1, r], pk_r.at[1, r], {"seq": peer}))
+    send_updates(0, (2,))
+    for c in range(1, NCH):
+        send_updates(c, ORDER)
+    og_s[...] = og[...].astype(F32) * gain_e
+
+    for copy in pk_in:
+        arrive(copy)
+    totals = jnp.concatenate([pk[k // SIDE, k % SIDE, 0:1, :] for k in range(16)], axis=0)
     low16 = (iota((16, 16), 0) >= iota((16, 16), 1)).astype(F32)
     t_cum = jnp.dot(low16, totals, precision=HIGH, preferred_element_type=F32)
     t_e = jnp.dot(t_cum[:, :16], spread16, precision=HIGH, preferred_element_type=F32)
     for half in range(2):
         f0, s0 = first[half], second[half]
-        parent = jnp.concatenate([pk[at(half, f0, s), 0, 4:8, :] for s in range(SIDE)], axis=0)
-        onehot = (parent == iota((16, 128), 1).astype(F32)).astype(F32)
+        parent = jnp.concatenate([(pk[s, f0] if half == 0 else pk[f0, s])[4:8] for s in range(SIDE)], axis=0)
+        onehot = (parent[:, 32:48] == iota((16, 16), 1).astype(F32)).astype(F32)
         lo = half * HALF
         t_half = t_e[:, lo : lo + HALF]
-        t_par = jnp.dot(onehot[:, :16], t_half, precision=HIGH, preferred_element_type=F32)
-        p_col = parent[:, 0:1]
+        t_par = jnp.dot(onehot, t_half, precision=HIGH, preferred_element_type=F32)
+        p_col = parent[:, 32:33]
         for f in range(SIDE):
             j = at(half, f, s0)
             pick = (iota((16, HALF), 0) == j).astype(F32)
@@ -208,12 +229,12 @@
             w = jnp.where(p_col >= j.astype(F32), jnp.exp(jnp.minimum(t_par - t_j, 0.0)), 0.0)
             for s in range(SIDE):
                 wt[half, f, s, 0:4] = w[4 * s : 4 * s + 4]
-    stats = pk[0, 1]
+    stats = pk[0, 0]
     for k in range(1, 16):
-        stats = stats + pk[k, 1]
-    floor_count = jnp.maximum(stats[:, 0:1], 1.0)
-    mean = stats[:, 1:2] / floor_count
-    spread = jnp.sqrt(stats[:, 2:3] / floor_count - mean * mean + 1.0)
+        stats = stats + pk[k // SIDE, k % SIDE]
+    floor_count = jnp.maximum(stats[:, 64:65], 1.0)
+    mean = stats[:, 65:66] / floor_count
+    spread = jnp.sqrt(stats[:, 66:67] / floor_count - mean * mean + 1.0)
     mean_row = jnp.sum(table * mean, axis=0, keepdims=True)
     spread_row = jnp.sum(table * spread, axis=0, keepdims=True)
     adv_row = (returns - mean_row) / spread_row
@@ -272,7 +293,7 @@
             gated = (y_s[:, ws] + got * lift_e[:, ws]) * sz_s[:, ws]
             gated_s[:, ws] = gated
             squares = gated * gated
-            inner = og[:, ws].astype(F32) * gain_e[:, ws] * gated
+            inner = og_s[:, ws] * gated
             for k in range(CW // 128):
                 sq = sq + squares[:, 128 * k : 128 * k + 128]
                 al = al + inner[:, 128 * k : 128 * k + 128]
@@ -300,7 +321,7 @@
         for half in range(2):
             lo = half * HALF + c * CW
             ws = slice(lo, lo + CW)
-            dy = (push_c * (og[:, ws].astype(F32) * gain_e[:, ws]) - kappa_c * gated_s[:, ws]) * sz_s[:, ws]
+            dy = (push_c * og_s[:, ws] - kappa_c * gated_s[:, ws]) * sz_s[:, ws]
             dy_s[:, ws] = dy
             f0, s0 = first[half], second[half]
             dg[half, c, s0] = (dy * lift_e[:, ws]).astype(BF16)
@@ -402,7 +423,7 @@
             pltpu.SMEM((NB,), jnp.int32), V((1, BLOCK), jnp.int32), V((1, BLOCK), F32),
             V((BLOCK, CH), BF16),
             dma((15,)),
-            V((16, 2, 8, 128), F32),
+            V((SIDE, SIDE, 8, 128), F32),
             V((8, 8, 128), F32),
             V((2, NCH, SIDE, STATE, CW), BF16),
             V((2, SIDE, BLOCK, STATE), BF16),
@@ -422,7 +443,8 @@
             V((BLOCK, CH), F32),
             V((BLOCK, CH), F32),
             V((BLOCK, CH), F32),
-            dma((16,)), dma((16,)), dma((8,)), dma((8,)),
+            V((BLOCK, CH), F32),
+            dma((2, SIDE)), dma((2, SIDE)), dma((8,)), dma((8,)),
             dma((2, NCH, SIDE)), dma((2, NCH, SIDE)),
             dma((2, SIDE)), dma((2, SIDE)),
             dma((2, NCH, SIDE)), dma((2, NCH, SIDE)),

time: 48.2 us -> 46 us (0.954)
  Pallas kernels: 47.4 us -> 45.2 us
    pallas_call x1, Pallas kernels: 46.4 us -> 44.2 us  [local(): pl.pallas_call(kernel, out_shape=(jax.ShapeDtypeStruct((BLOCK, CH), BF16)...]
where the time goes in v3:
time: 46 us; the launch traced here: 45.9 us
  Pallas kernels  45.2 us (98%)
  between operations  0.64 us (1%)
    pallas_call x1, Pallas kernels, local(): pl.pallas_call(kernel, out_shape=(jax.ShapeDtypeStruct((BLOCK, CH), BF16)...  44.2 us
    pallas_call x1, Pallas kernels, local(): pl.pallas_call(hand_over, out_shape=tuple((jax.ShapeDtypeStruct(r.shape,...  1.04 us

profile of v3, /device:TPU:0, one launch (start us, length us, event | category | flops | bytes accessed | tf_op | source)
XLA Modules:
  0.0 45.9 jit_solution(2130446432974033640)
XLA Ops:
  0.6 44.2 %shard_map.166 = (bf16[128,1024]{1,0:T(8,128)(2,1)S(1)}, bf16[128,1024]{1,0:T(8,128)(2,1)S(1)}, f32[128,1024]{1,0:T(8,128)S(1)}) custom-call(bf16[128,1024]{1,0:T(8,128)(2,1)} %px_h.1, bf16[128,128]{1,0:T(8,128)(2,1)} %pb_h.1, f32[16,128]{1,0:T(8,128)} %pdt_h.1, bf16[128,1024]{1,0:T(8,128)(2,1)} %bx_h.1, bf16[128,128]{1,0:T(8,128)(2,1)} %bb_h.1, ...), custom_call_target="tpu_custom_call" | custom-call | tf_op jit(solution)/shard_map/pallas_call | solution.py:409
  44.8 1.0 %shard_map.167 = (bf16[128,1024]{1,0:T(8,128)(2,1)}, bf16[128,1024]{1,0:T(8,128)(2,1)}, f32[128,1024]{1,0:T(8,128)}) custom-call(bf16[128,1024]{1,0:T(8,128)(2,1)S(1)} %get-tuple-element.6.a, bf16[128,1024]{1,0:T(8,128)(2,1)S(1)} %get-tuple-element.7.b, f32[128,1024]{1,0:T(8,128)S(1)} %get-tuple-element.8.c), custom_call_target="tpu_custom_call" | custom-call | tf_op jit(solution)/shard_map/pallas_call | solution.py:463

commit v4 on v3

--- a/solution.py
+++ b/solution.py
@@ -19,6 +19,7 @@
 CH = 1024
 HALF = 512
 NCH = 2
+EARLY = 1
 CW = HALF // NCH
 MESH_ID = pl.DeviceIdType.MESH
 F32 = jnp.float32
@@ -52,7 +53,8 @@
     px_h, pb_h, pdt_h, bx_h, bb_h, bc_h, bz_h, bdt_h, rate_h, skip_h, gain_h, par_h, gid_h, ret_h, og_h,
     out_o, grad_o, prompt_o,
     px, pb, pdt, bx, bb, bc, bz, bdt, rate, skip, gain, par, gid, ret, og, in_sem,
-    pk, ar, ug, cg, ct, yp, yr, dg, gp, gr, acc, wt, tail_e, lift_e, einv_e, smat, y_s, gated_s, sz_s, dy_s, og_s,
+    pk, ar, ug, cg, ct, yp, yr, dg, gp, gr, acc, wt, tail_e, lift_e, einv_e, smat, y_s, gated_s, sz_s, dy_s, og_s, pg, qg, sg, sg_c,
+    pg_s, pg_r, qg_s, qg_r, sg_s, sg_r,
     pk_s, pk_r, ar_s, ar_r, u_s, u_r, c_s, c_r, y_ss, y_rs, d_s, d_r, g_s, g_r,
 ):
     seq = lax.axis_index("seq")
@@ -239,6 +241,19 @@
     spread_row = jnp.sum(table * spread, axis=0, keepdims=True)
     adv_row = (returns - mean_row) / spread_row
 
+    def send_along(buf, s_sem, r_sem, half, c, distances):
+        copies = {}
+        s0 = second[half]
+        for r in distances:
+            copies[r] = send(
+                buf.at[half, c, s0],
+                buf.at[half, c, s0],
+                s_sem.at[half, c, r],
+                r_sem.at[half, c, r],
+                {"seq": at(half, first[half], (s0 + r) % SIDE)},
+            )
+        return copies
+
     for half in range(2):
         for copy in c_in[half]:
             arrive(copy)
@@ -275,6 +290,14 @@
                         y_s[:, lo : lo + CW] = y_s[:, lo : lo + CW] + part * lift_e[:, lo : lo + CW]
             y_in[half].append(copies)
 
+    p_in, q_in = [[], []], [[], []]
+    for c in range(EARLY):
+        for half in range(2):
+            lo = half * HALF + c * CW
+            ws = slice(lo, lo + CW)
+            s0 = second[half]
+            pg[half, c, s0] = (og_s[:, ws] * sz_s[:, ws] * lift_e[:, ws]).astype(BF16)
+
     for half in range(2):
         for s in range(SIDE):
             ct[half, s] = cg[half, s].astype(F32).T.astype(BF16)
@@ -292,6 +315,8 @@
                 got = v if got is None else got + v
             gated = (y_s[:, ws] + got * lift_e[:, ws]) * sz_s[:, ws]
             gated_s[:, ws] = gated
+            if c < EARLY:
+                qg[half, c, second[half]] = (gated * sz_s[:, ws] * lift_e[:, ws]).astype(BF16)
             squares = gated * gated
             inner = og_s[:, ws] * gated
             for k in range(CW // 128):
@@ -303,6 +328,10 @@
     ar_in = [
         send(ar.at[head], ar.at[head], ar_s.at[r], ar_r.at[r], {"head": (head + r) % 8}) for r in (4, 3, 5, 2, 6, 7, 1)
     ]
+    for c in range(EARLY):
+        for half in range(2):
+            q_in[half].append(send_along(qg, qg_s, qg_r, half, c, (2,)))
+            p_in[half].append(send_along(pg, pg_s, pg_r, half, c, (2,)))
     for copy in ar_in:
         arrive(copy)
     sums = ar[0]
@@ -313,6 +342,19 @@
     kappa = scale * scale * scale * along / (HEADS * HEAD_DIM)
     sub128 = iota((128, 128), 0)
     rows = jnp.where(sub128 == 0, scale, jnp.where(sub128 == 1, scale * adv_row, jnp.where(sub128 == 2, kappa, 0.0)))
+    sg[0, yi] = rows[0:8]
+    sg[1, xi] = rows[0:8]
+    s_in = [{}, {}]
+    for r in (2,):
+        for half in range(2):
+            s0 = second[half]
+            s_in[half][r] = send(
+                sg.at[half, s0],
+                sg.at[half, s0],
+                sg_s.at[half, r],
+                sg_r.at[half, r],
+                {"seq": at(half, first[half], (s0 + r) % SIDE)},
+            )
     cols = rows.T
     scale_c, push_c, kappa_c = cols[:, 0:1], cols[:, 1:2], cols[:, 2:3]
 
@@ -325,16 +367,7 @@
             dy_s[:, ws] = dy
             f0, s0 = first[half], second[half]
             dg[half, c, s0] = (dy * lift_e[:, ws]).astype(BF16)
-            copies = {}
-            for r in ORDER:
-                copies[r] = send(
-                    dg.at[half, c, s0],
-                    dg.at[half, c, s0],
-                    d_s.at[half, c, r],
-                    d_r.at[half, c, r],
-                    {"seq": at(half, f0, (s0 + r) % SIDE)},
-                )
-            d_in[half].append(copies)
+            d_in[half].append(send_along(dg, d_s, d_r, half, c, (1, 3) if c < EARLY else ORDER))
 
     scores_t = smat[...].astype(F32).T.astype(BF16)
     for c in range(NCH):
@@ -350,11 +383,21 @@
         for half in range(2):
             f0, s0 = first[half], second[half]
             cs = slice(c * CW, (c + 1) * CW)
-            for n, r in enumerate((0, 1, 3, 2)):
+            for n, r in enumerate((0, 2, 1, 3) if c < EARLY else (0, 1, 3, 2)):
                 s = (s0 + r) % SIDE
-                if r:
-                    arrive(d_in[half][c][(SIDE - r) % SIDE])
-                d = dg[half, c, s].astype(F32)
+                back = (SIDE - r) % SIDE
+                if r == 2 and c < EARLY:
+                    if c == 0:
+                        arrive(s_in[half][back])
+                        sg_c[half] = jnp.concatenate([sg[half, s], jnp.zeros((120, 128), F32)], axis=0).T
+                    arrive(p_in[half][c][back])
+                    arrive(q_in[half][c][back])
+                    d = sg_c[half, :, 1:2] * pg[half, c, s].astype(F32)
+                    d = d - sg_c[half, :, 2:3] * qg[half, c, s].astype(F32)
+                else:
+                    if r:
+                        arrive(d_in[half][c][back])
+                    d = dg[half, c, s].astype(F32)
                 copies = {}
                 for q in (2, 1, 3, 0):
                     f = (f0 + q) % SIDE
@@ -444,6 +487,13 @@
             V((BLOCK, CH), F32),
             V((BLOCK, CH), F32),
             V((BLOCK, CH), F32),
+            V((2, EARLY, SIDE, BLOCK, CW), BF16),
+            V((2, EARLY, SIDE, BLOCK, CW), BF16),
+            V((2, SIDE, 8, 128), F32),
+            V((2, BLOCK, 128), F32),
+            dma((2, EARLY, SIDE)), dma((2, EARLY, SIDE)),
+            dma((2, EARLY, SIDE)), dma((2, EARLY, SIDE)),
+            dma((2, SIDE)), dma((2, SIDE)),
             dma((2, SIDE)), dma((2, SIDE)), dma((8,)), dma((8,)),
             dma((2, NCH, SIDE)), dma((2, NCH, SIDE)),
             dma((2, SIDE)), dma((2, SIDE)),

time: 46 us -> 45.1 us (0.980)
  Pallas kernels: 45.2 us -> 44.3 us
    pallas_call x1, Pallas kernels: 44.2 us -> 43.3 us  [local(): pl.pallas_call(kernel, out_shape=(jax.ShapeDtypeStruct((BLOCK, CH), BF16)...]
where the time goes in v4:
time: 45.1 us; the launch traced here: 45 us
  Pallas kernels  44.3 us (98%)
  between operations  0.64 us (1%)
    pallas_call x1, Pallas kernels, local(): pl.pallas_call(kernel, out_shape=(jax.ShapeDtypeStruct((BLOCK, CH), BF16)...  43.3 us
    pallas_call x1, Pallas kernels, local(): pl.pallas_call(hand_over, out_shape=tuple((jax.ShapeDtypeStruct(r.shape,...  1.04 us

profile of v4, /device:TPU:0, one launch (start us, length us, event | category | flops | bytes accessed | tf_op | source)
XLA Modules:
  0.0 45.0 jit_solution(602506526586593927)
XLA Ops:
  0.6 43.3 %shard_map.166 = (bf16[128,1024]{1,0:T(8,128)(2,1)S(1)}, bf16[128,1024]{1,0:T(8,128)(2,1)S(1)}, f32[128,1024]{1,0:T(8,128)S(1)}) custom-call(bf16[128,1024]{1,0:T(8,128)(2,1)} %px_h.1, bf16[128,128]{1,0:T(8,128)(2,1)} %pb_h.1, f32[16,128]{1,0:T(8,128)} %pdt_h.1, bf16[128,1024]{1,0:T(8,128)(2,1)} %bx_h.1, bf16[128,128]{1,0:T(8,128)(2,1)} %bb_h.1, ...), custom_call_target="tpu_custom_call" | custom-call | tf_op jit(solution)/shard_map/pallas_call | solution.py:452
  43.9 1.0 %shard_map.167 = (bf16[128,1024]{1,0:T(8,128)(2,1)}, bf16[128,1024]{1,0:T(8,128)(2,1)}, f32[128,1024]{1,0:T(8,128)}) custom-call(bf16[128,1024]{1,0:T(8,128)(2,1)S(1)} %get-tuple-element.6.a, bf16[128,1024]{1,0:T(8,128)(2,1)S(1)} %get-tuple-element.7.b, f32[128,1024]{1,0:T(8,128)S(1)} %get-tuple-element.8.c), custom_call_target="tpu_custom_call" | custom-call | tf_op jit(solution)/shard_map/pallas_call | solution.py:513

commit v5 on v4

--- a/solution.py
+++ b/solution.py
@@ -75,6 +75,8 @@
             loads[name].wait()
 
     barrier = pltpu.get_barrier_semaphore()
+    for r in range(1, 8):
+        pl.semaphore_signal(barrier, inc=1, device_id={"head": (head + r) % 8}, device_id_type=MESH_ID)
     for r in range(1, SIDE):
         pl.semaphore_signal(
             barrier, inc=1, device_id={"seq": yi * SIDE + (xi + r) % SIDE}, device_id_type=MESH_ID
@@ -82,8 +84,6 @@
         pl.semaphore_signal(
             barrier, inc=1, device_id={"seq": (yi + r) % SIDE * SIDE + xi}, device_id_type=MESH_ID
         )
-    for r in range(1, 8):
-        pl.semaphore_signal(barrier, inc=1, device_id={"head": (head + r) % 8}, device_id_type=MESH_ID)
 
     first = (xi, yi)
     second = (yi, xi)
@@ -436,10 +436,15 @@
 PIECES = 4
 
 
-def hand_over(a, b, c, a_out, b_out, c_out):
-    a_out[...] = a[...]
-    b_out[...] = b[...]
-    c_out[...] = c[...]
+def hand_over(a, b, c, a_out, b_out, c_out, sem):
+    copies = [
+        pltpu.make_async_copy(src, dst, sem.at[n])
+        for n, (src, dst) in enumerate(((c, c_out), (a, a_out), (b, b_out)))
+    ]
+    for copy in copies:
+        copy.start()
+    for copy in copies:
+        copy.wait()
 
 
 def local(
@@ -514,7 +519,8 @@
         hand_over,
         out_shape=tuple(jax.ShapeDtypeStruct(r.shape, r.dtype) for r in results),
         in_specs=[vm] * 3,
-        out_specs=(vm,) * 3,
+        out_specs=(hbm,) * 3,
+        scratch_shapes=[dma((3,))],
         compiler_params=pltpu.CompilerParams(vmem_limit_bytes=16 * 2**20),
     )(*results)
 

time: 45.1 us -> 44.8 us (level)
  no operation moved by 1% of the time
where the time goes in v5:
time: 44.8 us; the launch traced here: 44.7 us
  Pallas kernels  44 us (98%)
  between operations  0.64 us (1%)
    pallas_call x1, Pallas kernels, local(): pl.pallas_call(kernel, out_shape=(jax.ShapeDtypeStruct((BLOCK, CH), BF16)...  43 us
    pallas_call x1, Pallas kernels, local(): pl.pallas_call(hand_over, out_shape=tuple((jax.ShapeDtypeStruct(r.shape,...  0.99 us

profile of v5, /device:TPU:0, one launch (start us, length us, event | category | flops | bytes accessed | tf_op | source)
XLA Modules:
  0.0 44.7 jit_solution(6214629718668279732)
XLA Ops:
  0.6 43.0 %shard_map.166 = (bf16[128,1024]{1,0:T(8,128)(2,1)S(1)}, bf16[128,1024]{1,0:T(8,128)(2,1)S(1)}, f32[128,1024]{1,0:T(8,128)S(1)}) custom-call(bf16[128,1024]{1,0:T(8,128)(2,1)} %px_h.1, bf16[128,128]{1,0:T(8,128)(2,1)} %pb_h.1, f32[16,128]{1,0:T(8,128)} %pdt_h.1, bf16[128,1024]{1,0:T(8,128)(2,1)} %bx_h.1, bf16[128,128]{1,0:T(8,128)(2,1)} %bb_h.1, ...), custom_call_target="tpu_custom_call" | custom-call | tf_op jit(solution)/shard_map/pallas_call | solution.py:457
  43.7 1.0 %shard_map.167 = (bf16[128,1024]{1,0:T(8,128)(2,1)}, bf16[128,1024]{1,0:T(8,128)(2,1)}, f32[128,1024]{1,0:T(8,128)}) custom-call(bf16[128,1024]{1,0:T(8,128)(2,1)S(1)} %get-tuple-element.6.a, bf16[128,1024]{1,0:T(8,128)(2,1)S(1)} %get-tuple-element.7.b, f32[128,1024]{1,0:T(8,128)S(1)} %get-tuple-element.8.c), custom_call_target="tpu_custom_call" | custom-call | tf_op jit(solution)/shard_map/pallas_call | solution.py:518

commit v6 on v5

--- a/solution.py
+++ b/solution.py
@@ -326,7 +326,7 @@
     al_row = jnp.sum(al.T, axis=0, keepdims=True)
     ar[head] = jnp.where(sub == 0, sq_row, jnp.where(sub == 1, al_row, 0.0))
     ar_in = [
-        send(ar.at[head], ar.at[head], ar_s.at[r], ar_r.at[r], {"head": (head + r) % 8}) for r in (4, 3, 5, 2, 6, 7, 1)
+        send(ar.at[head], ar.at[head], ar_s.at[r], ar_r.at[r], {"head": (head + r) % 8}) for r in (4, 5, 3, 6, 2, 7, 1)
     ]
     for c in range(EARLY):
         for half in range(2):
@@ -367,7 +367,7 @@
             dy_s[:, ws] = dy
             f0, s0 = first[half], second[half]
             dg[half, c, s0] = (dy * lift_e[:, ws]).astype(BF16)
-            d_in[half].append(send_along(dg, d_s, d_r, half, c, (1, 3) if c < EARLY else ORDER))
+            d_in[half].append(send_along(dg, d_s, d_r, half, c, (1, 3) if c < EARLY else (2, 1, 3)))
 
     scores_t = smat[...].astype(F32).T.astype(BF16)
     for c in range(NCH):

time: 44.8 us -> 45.6 us (1.018)
  Pallas kernels: 44 us -> 44.8 us
    pallas_call x1, Pallas kernels: 43 us -> 43.8 us  [local(): pl.pallas_call(kernel, out_shape=(jax.ShapeDtypeStruct((BLOCK, CH), BF16)...]
where the time goes in v6:
time: 45.6 us; the launch traced here: 45.4 us
  Pallas kernels  44.8 us (98%)
  between operations  0.64 us (1%)
    pallas_call x1, Pallas kernels, local(): pl.pallas_call(kernel, out_shape=(jax.ShapeDtypeStruct((BLOCK, CH), BF16)...  43.8 us
    pallas_call x1, Pallas kernels, local(): pl.pallas_call(hand_over, out_shape=tuple((jax.ShapeDtypeStruct(r.shape,...  0.99 us

profile of v6, /device:TPU:0, one launch (start us, length us, event | category | flops | bytes accessed | tf_op | source)
XLA Modules:
  0.0 45.4 jit_solution(6588877868958310687)
XLA Ops:
  0.6 43.8 %shard_map.166 = (bf16[128,1024]{1,0:T(8,128)(2,1)S(1)}, bf16[128,1024]{1,0:T(8,128)(2,1)S(1)}, f32[128,1024]{1,0:T(8,128)S(1)}) custom-call(bf16[128,1024]{1,0:T(8,128)(2,1)} %px_h.1, bf16[128,128]{1,0:T(8,128)(2,1)} %pb_h.1, f32[16,128]{1,0:T(8,128)} %pdt_h.1, bf16[128,1024]{1,0:T(8,128)(2,1)} %bx_h.1, bf16[128,128]{1,0:T(8,128)(2,1)} %bb_h.1, ...), custom_call_target="tpu_custom_call" | custom-call | tf_op jit(solution)/shard_map/pallas_call | solution.py:457
  44.5 1.0 %shard_map.167 = (bf16[128,1024]{1,0:T(8,128)(2,1)}, bf16[128,1024]{1,0:T(8,128)(2,1)}, f32[128,1024]{1,0:T(8,128)}) custom-call(bf16[128,1024]{1,0:T(8,128)(2,1)S(1)} %get-tuple-element.6.a, bf16[128,1024]{1,0:T(8,128)(2,1)S(1)} %get-tuple-element.7.b, f32[128,1024]{1,0:T(8,128)S(1)} %get-tuple-element.8.c), custom_call_target="tpu_custom_call" | custom-call | tf_op jit(solution)/shard_map/pallas_call | solution.py:518
